TPU v7x, 32 devices: a whole 2x2x4 slice. The times are simulated.
32 devices in a mesh: fsdp: 8 (over z, core), ctx: 4 (over y, x).
Axes of the slice: x: 2, y: 2, z: 4, core: 2. Of those that a mesh axis runs over, the one named last changes fastest.
Arguments:
- hidden_in: bfloat16 [16384, 1024], P(('fsdp', 'ctx')), may hold values from -6 to 6
- seg_ids: int32 [16384], P(('fsdp', 'ctx')), may hold values from 0 to 4, as said below
- gain_mixer: float32 [1024], replicated, may hold values from 0.5 to 1.5
- gain_ffn: float32 [1024], replicated, may hold values from 0.5 to 1.5
- w_in: bfloat16 [1024, 3352], P('fsdp'), may hold values from -0.1875 to 0.1875
- w_qkv: bfloat16 [1024, 768], P('fsdp'), may hold values from -0.1875 to 0.1875
- w_attn_out: bfloat16 [512, 1024], P('fsdp'), may hold values from -4 to 4
- w_ssm_out: bfloat16 [1536, 1024], P('fsdp'), may hold values from -0.01953125 to 0.01953125
- w_gate_up: bfloat16 [1024, 4096], P('fsdp'), may hold values from -0.1875 to 0.1875
- w_down: bfloat16 [2048, 1024], P('fsdp'), may hold values from -0.125 to 0.125
- dt_bias: float32 [24], replicated, may hold values from -5 to -2.5
- a_log: float32 [24], replicated, may hold values from -7 to 0
- d_skip: float32 [24], replicated, may hold values from 0.5 to 1.5
- out_grad: bfloat16 [16384, 1024], P(('fsdp', 'ctx')), may hold values from -6 to 6
Outputs:
- output: bfloat16 [16384, 1024], P(('fsdp', 'ctx'))
- grad_in: float32 [16384, 1024], P(('fsdp', 'ctx'))
- grad_gain_mixer: float32 [1024], P('fsdp')
- grad_gain_ffn: float32 [1024], P('fsdp')
- grad_w_in: float32 [1024, 3352], P('fsdp')
- grad_w_qkv: float32 [1024, 768], P('fsdp')
- grad_w_attn_out: float32 [512, 1024], P('fsdp')
- grad_w_ssm_out: float32 [1536, 1024], P('fsdp')
- grad_w_gate_up: float32 [1024, 4096], P('fsdp')
- grad_w_down: float32 [2048, 1024], P('fsdp')
- grad_dt_bias: float32 [24], replicated
- grad_a_log: float32 [24], replicated
- grad_d_skip: float32 [24], replicated
Inputs may be any that keep to these rules, and one draw needn't show every extreme that they name: `seg_ids`: within each group of 2048 tokens the ids start at 0, never fall and rise by one at a sequence's start; every group holds ids 0 to 4; sequences 0 and 1 lie within the group's first 512 tokens, sequences 3 and 4 within its last 512, so sequence 2 runs from the first of the group's devices to its last.
All inputs are finite; a program needn't handle non-finite values.
Results may differ from a plain program's by a relative error of at most 0.02.
Values may be sent and summed in bfloat16 or wider, within the bound.
No kernel may reach another device: no remote copies, remote signals or barrier semaphores. Data moves between devices by JAX's collectives and lax.ppermute only.
A program may use at most 384 MiB of HBM per device.

v0:
```python
import jax
import jax.numpy as jnp
from jax import lax
from jax.sharding import PartitionSpec as P

FF = 2048
QUERY_HEADS = 8
KEY_VALUE_HEADS = 2
HEAD_WIDTH = 64
MH = 24
PD = 64
ST = 128


EPS = 1e-05
ROPE_BASE = 100000000000.0
HIGH = lax.Precision.HIGHEST


def entering(array, axis, combine, identity):
    count, position = (lax.axis_size(axis), lax.axis_index(axis))
    everything = jax.tree.map(
        lambda part, kind: lax.all_gather(part.astype(kind), axis),
        array,
        (jnp.bfloat16, jnp.bfloat16),
    )
    start = jax.tree.map(
        lambda part, zero: jnp.broadcast_to(jnp.asarray(zero, part.dtype), part.shape),
        array,
        identity,
    )

    def entering_turn(k, before):
        reached = k < position
        new = combine(
            before, jax.tree.map(lambda part, own: part[k].astype(own.dtype), everything, array)
        )
        return jax.tree.map(lambda a, b: jnp.where(reached, a, b), new, before)

    return lax.fori_loop(0, count, entering_turn, start)


def prefix(array, axis, combine, identity):
    count, position = (lax.axis_size(axis), lax.axis_index(axis))
    everything = jax.tree.map(
        lambda part, kind: lax.all_gather(part.astype(kind), axis),
        array,
        jax.tree.map(lambda a: jnp.bfloat16 if a.dtype == jnp.float32 else a.dtype, array),
    )
    start = jax.tree.map(
        lambda part, zero: jnp.broadcast_to(jnp.asarray(zero, part.dtype), part.shape),
        array,
        identity,
    )

    def prefix_turn(k, before):
        at = count - 1 - k
        reached = at > position
        new = combine(
            before, jax.tree.map(lambda part, own: part[at].astype(own.dtype), everything, array)
        )
        return jax.tree.map(lambda a, b: jnp.where(reached, a, b), new, before)

    return lax.fori_loop(0, count, prefix_turn, start)


def rms_forward(value_rows, gain):
    inverse = lax.rsqrt(jnp.mean(value_rows * value_rows, axis=-1, keepdims=True) + EPS)
    return (value_rows * inverse * gain, inverse)


def rms_backward(value_rows, inverse, gain, grad):
    weighted = grad * gain
    gain_grad = jnp.sum(grad * value_rows * inverse, axis=0)
    inner = jnp.mean(weighted * value_rows, axis=-1, keepdims=True)
    return (inverse * weighted - value_rows * inverse * inverse * inverse * inner, gain_grad)


def rope_tables(positions):
    half = HEAD_WIDTH // 2
    freqs = ROPE_BASE ** (-(jnp.arange(half, dtype=jnp.float32) * 2.0) / HEAD_WIDTH)
    angles = positions.astype(jnp.float32)[:, None] * freqs[None, :]
    return (jnp.cos(angles), jnp.sin(angles))


def apply_rotary(value_rows, cosine_table, sine_table):
    half = value_rows.shape[-1] // 2
    leading = value_rows[..., :half]
    trailing = value_rows[..., half:]
    cos_part = cosine_table[:, None, :]
    sin_part = sine_table[:, None, :]
    return jnp.concatenate(
        [leading * cos_part - trailing * sin_part, trailing * cos_part + leading * sin_part],
        axis=-1,
    )


def rotate_back(grads, cosine_table, sine_table):
    half = grads.shape[-1] // 2
    leading = grads[..., :half]
    trailing = grads[..., half:]
    cos_part = cosine_table[:, None, :]
    sin_part = sine_table[:, None, :]
    return jnp.concatenate(
        [leading * cos_part + trailing * sin_part, trailing * cos_part - leading * sin_part],
        axis=-1,
    )


def ssd_blocks(x_heads, b_vals, c_vals, steps, logd, segment_labels, span):
    count = x_heads.shape[0]
    heads = x_heads.shape[1]
    dims = x_heads.shape[2]
    states = b_vals.shape[1]
    block_count = count // span
    order = jnp.arange(span)
    lower = order[:, None] >= order[None, :]

    def step(carry, item):
        state, last = carry
        x_block, b_block, c_block, dt_block, log_block, seg_block = item
        cumul = jnp.cumsum(log_block, axis=0)
        same = lower & (seg_block[:, None] == seg_block[None, :])
        gap = jnp.where(same[:, :, None], cumul[:, None, :] - cumul[None, :, :], 0.0)
        decay = jnp.where(same[:, :, None], jnp.exp(gap), 0.0)
        inner = jnp.dot(c_block, b_block.T, precision=HIGH)
        mixing = decay * inner[:, :, None]
        scaled = x_block * dt_block[:, :, None]
        result = jnp.einsum("tsh,shp->thp", mixing, scaled, precision=HIGH)
        keep = jnp.exp(cumul) * (seg_block == last).astype(jnp.float32)[:, None]
        result = result + keep[:, :, None] * jnp.einsum(
            "tn,hpn->thp", c_block, state, precision=HIGH
        )
        tail = (seg_block == seg_block[-1]).astype(jnp.float32)[:, None] * jnp.exp(
            cumul[-1][None, :] - cumul
        )
        fresh = jnp.einsum("sh,shp,sn->hpn", tail * dt_block, x_block, b_block, precision=HIGH)
        state = keep[-1][:, None, None] * state + fresh
        return ((state, seg_block[-1]), result)

    init = (jnp.zeros((heads, dims, states), jnp.float32), jnp.full((), -1, jnp.int32))
    items = (
        x_heads.reshape(block_count, span, heads, dims),
        b_vals.reshape(block_count, span, states),
        c_vals.reshape(block_count, span, states),
        steps.reshape(block_count, span, heads),
        logd.reshape(block_count, span, heads),
        segment_labels.reshape(block_count, span),
    )
    (state, last), results = lax.scan(step, init, items)
    return (results.reshape(count, heads, dims), state)


def mamba_core(x_heads, b_vals, c_vals, dt_raw, dt_bias, a_log, segment_labels, prev_seg, span):
    steps = jax.nn.softplus(dt_raw + dt_bias)
    logd = -steps * jnp.exp(a_log)
    local, end_state = ssd_blocks(x_heads, b_vals, c_vals, steps, logd, segment_labels, span)
    log_cum = jnp.cumsum(logd, axis=0)
    flow = jnp.exp(log_cum[-1]) * (segment_labels[-1] == prev_seg).astype(jnp.float32)
    return (local, end_state, flow, log_cum)


def chain_combine(earlier, later):
    return (earlier[0] * later[0], earlier[1] * later[0][:, None, None] + later[1])


def score_block(query_rows, key_block, seg_block, index_block, query_seg, query_index):
    scores = jnp.einsum(
        "qgrd,kgd->qgrk", query_rows, key_block, preferred_element_type=jnp.float32
    ) * HEAD_WIDTH ** (-0.5)
    allowed = (query_seg[:, None] == seg_block[None, :]) & (
        index_block[None, :] <= query_index[:, None]
    )
    return jnp.where(allowed[:, None, None, :], scores, -1e30)


def key_blocks(every_key_row, every_value_row, key_seg, block_width):
    total_length = every_key_row.shape[0]
    block_count = total_length // block_width
    return (
        every_key_row.reshape(block_count, block_width, KEY_VALUE_HEADS, HEAD_WIDTH),
        every_value_row.reshape(block_count, block_width, KEY_VALUE_HEADS, HEAD_WIDTH),
        key_seg.reshape(block_count, block_width),
        jnp.arange(total_length, dtype=jnp.int32).reshape(block_count, block_width),
    )


def attend_forward(
    query_rows, every_key_row, every_value_row, query_seg, query_index, key_seg, block_width
):
    items = key_blocks(every_key_row, every_value_row, key_seg, block_width)
    shape = query_rows.shape[:3]

    def sweep(carry, item):
        top, mass = carry
        key_block, value_block, seg_block, index_block = item
        scores = score_block(query_rows, key_block, seg_block, index_block, query_seg, query_index)
        fresh = jnp.maximum(top, jnp.max(scores, axis=-1))
        mass = mass * jnp.exp(top - fresh) + jnp.sum(jnp.exp(scores - fresh[..., None]), axis=-1)
        return ((fresh, mass), None)

    start = (jnp.full(shape, -1e30, jnp.float32), jnp.zeros(shape, jnp.float32))
    (top, mass), unused = lax.scan(sweep, start, items)
    lse = top + jnp.log(mass)

    def collect(rounded, item):
        key_block, value_block, seg_block, index_block = item
        scores = score_block(query_rows, key_block, seg_block, index_block, query_seg, query_index)
        probs = jnp.exp(scores - lse[..., None])
        rounded = rounded + jnp.einsum(
            "qgrk,kgd->qgrd",
            probs.astype(jnp.bfloat16),
            value_block,
            preferred_element_type=jnp.float32,
        )
        return (rounded, None)

    empty = jnp.zeros(query_rows.shape, jnp.float32)
    rounded, unused = lax.scan(collect, empty, items)
    return (lse, rounded)


def attend_backward(
    query_rows,
    every_key_row,
    every_value_row,
    query_seg,
    query_index,
    key_seg,
    block_width,
    lse,
    grad_out,
    delta,
):
    items = key_blocks(every_key_row, every_value_row, key_seg, block_width)
    scale = HEAD_WIDTH ** (-0.5)

    def sweep(carry, item):
        key_block, value_block, seg_block, index_block = item
        scores = score_block(query_rows, key_block, seg_block, index_block, query_seg, query_index)
        probs = jnp.exp(scores - lse[..., None])
        value_gradient = jnp.einsum(
            "qgrk,qgrd->kgd",
            probs.astype(jnp.bfloat16),
            grad_out,
            preferred_element_type=jnp.float32,
        )
        prob_grad = jnp.einsum(
            "qgrd,kgd->qgrk", grad_out, value_block, preferred_element_type=jnp.float32
        )
        score_grad = (probs * (prob_grad - delta[..., None])).astype(jnp.bfloat16)
        carry = (
            carry
            + jnp.einsum(
                "qgrk,kgd->qgrd", score_grad, key_block, preferred_element_type=jnp.float32
            )
            * scale
        )
        key_grad = (
            jnp.einsum("qgrk,qgrd->kgd", score_grad, query_rows, preferred_element_type=jnp.float32)
            * scale
        )
        return (carry, (key_grad, value_gradient))

    query_gradient, (key_gradients, value_gradients) = lax.scan(
        sweep, jnp.zeros(query_rows.shape, jnp.float32), items
    )
    total_length = every_key_row.shape[0]
    return (
        query_gradient,
        key_gradients.reshape(total_length, KEY_VALUE_HEADS, HEAD_WIDTH),
        value_gradients.reshape(total_length, KEY_VALUE_HEADS, HEAD_WIDTH),
    )


def shards(
    hidden_in,
    seg_ids,
    gain_mixer,
    gain_ffn,
    w_in,
    w_qkv,
    w_attn_out,
    w_ssm_out,
    w_gate_up,
    w_down,
    dt_bias,
    a_log,
    d_skip,
    out_grad,
):
    token_rows = hidden_in.shape[0]
    place = lax.axis_index("ctx")
    ssm_width = MH * PD
    span = min(256, token_rows)
    query_groups = QUERY_HEADS // KEY_VALUE_HEADS
    full_in, full_qkv, full_gate_up, full_attn_out, full_ssm_out, full_down = (
        lax.all_gather(w_in, "fsdp", axis=0, tiled=True),
        lax.all_gather(w_qkv, "fsdp", axis=0, tiled=True),
        lax.all_gather(w_gate_up, "fsdp", axis=0, tiled=True),
        lax.all_gather(w_attn_out, "fsdp", axis=0, tiled=True),
        lax.all_gather(w_ssm_out, "fsdp", axis=0, tiled=True),
        lax.all_gather(w_down, "fsdp", axis=0, tiled=True),
    )
    seg_all = lax.all_gather(seg_ids, "ctx", axis=0, tiled=True)
    total_length = seg_all.shape[0]
    block_width = min(1024, total_length)
    order_all = jnp.arange(total_length, dtype=jnp.int32)
    earlier_seg = jnp.concatenate([jnp.full((1,), -1, jnp.int32), seg_all[:-1]])
    starts = lax.cummax(jnp.where(seg_all != earlier_seg, order_all, 0), axis=0)
    offset = place * token_rows
    query_index = offset + jnp.arange(token_rows, dtype=jnp.int32)
    positions = query_index - lax.dynamic_slice_in_dim(starts, offset, token_rows)
    before_first = lax.dynamic_slice_in_dim(seg_all, jnp.maximum(offset - 1, 0), 1)[0]
    prev_seg = jnp.where(place > 0, before_first, -1)
    inputs = hidden_in.astype(jnp.float32)
    normed, inverse_mixer = rms_forward(inputs, gain_mixer)
    normed_low = normed.astype(jnp.bfloat16)
    projected = jnp.dot(normed_low, full_in, preferred_element_type=jnp.float32)
    gate_z = projected[:, :ssm_width]
    ssm_x = projected[:, ssm_width : 2 * ssm_width].astype(jnp.bfloat16)
    ssm_b = projected[:, 2 * ssm_width : 2 * ssm_width + ST].astype(jnp.bfloat16)
    ssm_c = projected[:, 2 * ssm_width + ST : 2 * ssm_width + 2 * ST].astype(jnp.bfloat16)
    dt_raw = projected[:, 2 * ssm_width + 2 * ST :]
    query_key_value = jnp.dot(normed_low, full_qkv, preferred_element_type=jnp.float32)
    cosine_table, sine_table = rope_tables(positions)
    query_reduced = apply_rotary(
        query_key_value[:, : QUERY_HEADS * HEAD_WIDTH].reshape(token_rows, QUERY_HEADS, HEAD_WIDTH),
        cosine_table,
        sine_table,
    ).astype(jnp.bfloat16)
    key_low = apply_rotary(
        query_key_value[
            :, QUERY_HEADS * HEAD_WIDTH : (QUERY_HEADS + KEY_VALUE_HEADS) * HEAD_WIDTH
        ].reshape(token_rows, KEY_VALUE_HEADS, HEAD_WIDTH),
        cosine_table,
        sine_table,
    ).astype(jnp.bfloat16)
    value_reduced = (
        query_key_value[:, (QUERY_HEADS + KEY_VALUE_HEADS) * HEAD_WIDTH :]
        .reshape(token_rows, KEY_VALUE_HEADS, HEAD_WIDTH)
        .astype(jnp.bfloat16)
    )
    every_key_row, every_value_row = (
        lax.all_gather(key_low, "ctx", axis=0, tiled=True),
        lax.all_gather(value_reduced, "ctx", axis=0, tiled=True),
    )
    query_rows = query_reduced.reshape(token_rows, KEY_VALUE_HEADS, query_groups, HEAD_WIDTH)
    lse, attended_rows = attend_forward(
        query_rows, every_key_row, every_value_row, seg_ids, query_index, seg_all, block_width
    )
    attended_low = attended_rows.reshape(token_rows, QUERY_HEADS * HEAD_WIDTH).astype(jnp.bfloat16)
    attn_branch = jnp.dot(attended_low, full_attn_out, preferred_element_type=jnp.float32)
    x_heads = ssm_x.astype(jnp.float32).reshape(token_rows, MH, PD)
    b_vals = ssm_b.astype(jnp.float32)
    c_vals = ssm_c.astype(jnp.float32)

    def mixer_core(x_heads, b_vals, c_vals, dt_raw, dt_bias, a_log):
        return mamba_core(x_heads, b_vals, c_vals, dt_raw, dt_bias, a_log, seg_ids, prev_seg, span)

    (local, end_state, flow, log_cum), core_back = jax.vjp(
        mixer_core, x_heads, b_vals, c_vals, dt_raw, dt_bias, a_log
    )
    identity = (jnp.ones_like(flow), jnp.zeros_like(end_state))
    flow_in, state_in = entering((flow, end_state), "ctx", chain_combine, identity)

    def finish(local, log_cum, c_vals, x_heads, gate_z, d_skip, state_in):
        entry = jnp.exp(log_cum) * (seg_ids == prev_seg).astype(jnp.float32)[:, None]
        carried = jnp.einsum("tn,hpn->thp", c_vals, state_in, precision=HIGH)
        mixed = local + entry[:, :, None] * carried + d_skip[None, :, None] * x_heads
        return (mixed * jax.nn.silu(gate_z.reshape(token_rows, MH, PD))).reshape(
            token_rows, ssm_width
        )

    gated, finish_back = jax.vjp(finish, local, log_cum, c_vals, x_heads, gate_z, d_skip, state_in)
    gated_low = gated.astype(jnp.bfloat16)
    ssm_branch = jnp.dot(gated_low, full_ssm_out, preferred_element_type=jnp.float32)
    middle = inputs + attn_branch + ssm_branch
    normed_ffn, inverse_ffn = rms_forward(middle, gain_ffn)
    normed_ffn_low = normed_ffn.astype(jnp.bfloat16)
    gate_up = jnp.dot(normed_ffn_low, full_gate_up, preferred_element_type=jnp.float32)
    gate_part = gate_up[:, :FF]
    up_part = gate_up[:, FF:]
    sigmoid_gate = jax.nn.sigmoid(gate_part)
    hidden_low = (gate_part * sigmoid_gate * up_part).astype(jnp.bfloat16)
    ffn_branch = jnp.dot(hidden_low, full_down, preferred_element_type=jnp.float32)
    output = (middle + ffn_branch).astype(jnp.bfloat16)
    grad_top = out_grad.astype(jnp.float32)
    down_grad = jnp.dot(hidden_low.T, out_grad, preferred_element_type=jnp.float32)
    hidden_grad = jnp.dot(out_grad, full_down.T, preferred_element_type=jnp.float32)
    gate_grad = hidden_grad * up_part * sigmoid_gate * (1.0 + gate_part * (1.0 - sigmoid_gate))
    up_grad = hidden_grad * gate_part * sigmoid_gate
    gate_up_grad_low = jnp.concatenate([gate_grad, up_grad], axis=1).astype(jnp.bfloat16)
    gate_up_w_grad = jnp.dot(normed_ffn_low.T, gate_up_grad_low, preferred_element_type=jnp.float32)
    normed_ffn_grad = jnp.dot(gate_up_grad_low, full_gate_up.T, preferred_element_type=jnp.float32)
    middle_part, gain_ffn_grad = rms_backward(middle, inverse_ffn, gain_ffn, normed_ffn_grad)
    middle_grad = grad_top + middle_part
    branch_low = middle_grad.astype(jnp.bfloat16)
    attn_out_grad = jnp.dot(attended_low.T, branch_low, preferred_element_type=jnp.float32)
    ssm_out_grad = jnp.dot(gated_low.T, branch_low, preferred_element_type=jnp.float32)
    attended_gradient = jnp.dot(
        branch_low, full_attn_out.T, preferred_element_type=jnp.float32
    ).astype(jnp.bfloat16)
    gated_grad = (
        jnp.dot(branch_low, full_ssm_out.T, preferred_element_type=jnp.float32)
        .astype(jnp.bfloat16)
        .astype(jnp.float32)
    )
    local_grad, log_cum_grad, c_grad_outer, x_grad_outer, gate_z_grad, d_skip_grad, state_grad = (
        finish_back(gated_grad)
    )
    flow_out, later_grad = prefix((flow, state_grad), "ctx", chain_combine, identity)
    flow_grad = jnp.sum(later_grad * state_in, axis=(1, 2))
    x_grad_inner, b_grad, c_grad_inner, dt_raw_grad, dt_bias_grad, a_log_grad = core_back(
        (local_grad, later_grad, flow_grad, log_cum_grad)
    )
    projected_grad_low = jnp.concatenate(
        [
            gate_z_grad,
            (x_grad_outer + x_grad_inner).reshape(token_rows, ssm_width),
            b_grad,
            c_grad_outer + c_grad_inner,
            dt_raw_grad,
        ],
        axis=1,
    ).astype(jnp.bfloat16)
    attended_head_gradient = attended_gradient.reshape(
        token_rows, KEY_VALUE_HEADS, query_groups, HEAD_WIDTH
    )
    delta = jnp.sum(attended_head_gradient.astype(jnp.float32) * attended_rows, axis=-1)
    query_gradient, key_gradients, value_gradients = attend_backward(
        query_rows,
        every_key_row,
        every_value_row,
        seg_ids,
        query_index,
        seg_all,
        block_width,
        lse,
        attended_head_gradient,
        delta,
    )
    key_grad, value_gradient = (
        lax.psum_scatter(
            key_gradients.astype(jnp.bfloat16), "ctx", scatter_dimension=0, tiled=True
        ).astype(jnp.float32),
        lax.psum_scatter(
            value_gradients.astype(jnp.bfloat16), "ctx", scatter_dimension=0, tiled=True
        ).astype(jnp.float32),
    )
    query_raw_grad = rotate_back(
        query_gradient.reshape(token_rows, QUERY_HEADS, HEAD_WIDTH), cosine_table, sine_table
    )
    unrotated_key_gradient = rotate_back(key_grad, cosine_table, sine_table)
    qkv_grad_low = jnp.concatenate(
        [
            query_raw_grad.reshape(token_rows, QUERY_HEADS * HEAD_WIDTH),
            unrotated_key_gradient.reshape(token_rows, KEY_VALUE_HEADS * HEAD_WIDTH),
            value_gradient.reshape(token_rows, KEY_VALUE_HEADS * HEAD_WIDTH),
        ],
        axis=1,
    ).astype(jnp.bfloat16)
    in_w_grad = jnp.dot(normed_low.T, projected_grad_low, preferred_element_type=jnp.float32)
    qkv_w_grad = jnp.dot(normed_low.T, qkv_grad_low, preferred_element_type=jnp.float32)
    normed_grad = jnp.dot(projected_grad_low, full_in.T, preferred_element_type=jnp.float32)
    normed_grad = normed_grad + jnp.dot(
        qkv_grad_low, full_qkv.T, preferred_element_type=jnp.float32
    )
    input_part, gain_mixer_grad = rms_backward(inputs, inverse_mixer, gain_mixer, normed_grad)
    input_grad = middle_grad + input_part
    gradients = (
        in_w_grad,
        qkv_w_grad,
        attn_out_grad,
        ssm_out_grad,
        gate_up_w_grad,
        down_grad,
        gain_mixer_grad,
        gain_ffn_grad,
    )
    shares = (
        lax.psum_scatter(
            gradients[0].astype(jnp.bfloat16), "fsdp", scatter_dimension=0, tiled=True
        ).astype(jnp.float32),
        lax.psum_scatter(
            gradients[1].astype(jnp.bfloat16), "fsdp", scatter_dimension=0, tiled=True
        ).astype(jnp.float32),
        lax.psum_scatter(
            gradients[2].astype(jnp.bfloat16), "fsdp", scatter_dimension=0, tiled=True
        ).astype(jnp.float32),
        lax.psum_scatter(
            gradients[3].astype(jnp.bfloat16), "fsdp", scatter_dimension=0, tiled=True
        ).astype(jnp.float32),
        lax.psum_scatter(
            gradients[4].astype(jnp.bfloat16), "fsdp", scatter_dimension=0, tiled=True
        ).astype(jnp.float32),
        lax.psum_scatter(
            gradients[5].astype(jnp.bfloat16), "fsdp", scatter_dimension=0, tiled=True
        ).astype(jnp.float32),
        lax.psum_scatter(
            gradients[6].astype(jnp.bfloat16), "fsdp", scatter_dimension=0, tiled=True
        ).astype(jnp.float32),
        lax.psum_scatter(
            gradients[7].astype(jnp.bfloat16), "fsdp", scatter_dimension=0, tiled=True
        ).astype(jnp.float32),
    )
    summed = (
        lax.psum(shares[0].astype(jnp.bfloat16), "ctx").astype(jnp.float32),
        lax.psum(shares[1].astype(jnp.bfloat16), "ctx").astype(jnp.float32),
        lax.psum(shares[2].astype(jnp.bfloat16), "ctx").astype(jnp.float32),
        lax.psum(shares[3].astype(jnp.bfloat16), "ctx").astype(jnp.float32),
        lax.psum(shares[4].astype(jnp.bfloat16), "ctx").astype(jnp.float32),
        lax.psum(shares[5].astype(jnp.bfloat16), "ctx").astype(jnp.float32),
        lax.psum(shares[6].astype(jnp.bfloat16), "ctx").astype(jnp.float32),
        lax.psum(shares[7].astype(jnp.bfloat16), "ctx").astype(jnp.float32),
    )
    head_sums = lax.psum((dt_bias_grad, a_log_grad, d_skip_grad), ("fsdp", "ctx"))
    return (
        output,
        input_grad,
        summed[6],
        summed[7],
        summed[0],
        summed[1],
        summed[2],
        summed[3],
        summed[4],
        summed[5],
        head_sums[0],
        head_sums[1],
        head_sums[2],
    )


def solution(mesh):
    return jax.shard_map(
        shards,
        mesh=mesh,
        in_specs=(
            P(("fsdp", "ctx"), None),
            P(("fsdp", "ctx")),
            P(),
            P(),
            P("fsdp", None),
            P("fsdp", None),
            P("fsdp", None),
            P("fsdp", None),
            P("fsdp", None),
            P("fsdp", None),
            P(),
            P(),
            P(),
            P(("fsdp", "ctx"), None),
        ),
        out_specs=(
            P(("fsdp", "ctx"), None),
            P(("fsdp", "ctx"), None),
            P("fsdp"),
            P("fsdp"),
            P("fsdp", None),
            P("fsdp", None),
            P("fsdp", None),
            P("fsdp", None),
            P("fsdp", None),
            P("fsdp", None),
            P(),
            P(),
            P(),
        ),
        check_vma=False,
    )
```

profile of v0, /device:TPU:0, one launch (start us, length us, event | category | flops | bytes accessed | tf_op | source)
XLA Modules:
  0.0 1303.7 jit_solution(14215825542039811942)
XLA Ops:
  12.4 69.9 %all-gather.17.cloned.1.call-done = bf16[1024,3352]{0,1:T(8,128)(2,1)} async-done(((bf16[128,3352]{0,1:T(8,128)(2,1)}), bf16[1024,3352]{0,1:T(8,128)(2,1)}) %all-gather.17.cloned.1.call-update) | async-done | bytes 6864912 | tf_op jit(solution)/shard_map/all_gather | solution.py:298
  82.2 6.6 fusion.258
  105.6 150.7 %while.154 = (s32[]{:T(128)}, f32[24,64,128]{2,1,0:T(8,128)}, s32[]{:T(128)}, f32[2,256,24,64]{1,0,3,2:T(2,128)}, pred[2,256,256,24]{2,3,1,0:T(8,128)(4,1)}, /*i...) while((s32[]{:T(128)}, f32[24,64,128]{2,1,0:T(8,128)}, ...), condition=%wide.region_12.13_spmd.clone, body=%wide.region_9.12_spmd.clone.sunk | while | flops 2533529600 | bytes 113260664 | solution.py:150
  122.5 7.2 fusion.397
  132.5 32.4 %dynamic_update_slice.294 = f32[2,256,24,64]{1,0,3,2:T(2,128)} dynamic-update-slice(f32[2,256,24,64]{1,0,3,2:T(2,128)} %get-tuple-element.3271, f32[1,256,24,64]{1,0,3,2:T(1,128)} %copy.458, s32[]{:T(128)S(6)} %copy.510, s32[]{:T(128)} %constant.322.clone.1..sunk.3, s32[]{:T(128)} %constant.322.clone.1..sunk.3, s32[]{:T(128)} %constant.322.clone.1..sunk.3) | dynamic-update-slice | bytes 3145732 | tf_op jit(solution)/shard_map/jvp()/while/body/jit(dynamic_update_index_in_dim)/dynamic_update_slice | solution.py:150
  167.2 8.6 multiply_dynamic-update-slice_fusion.3
  198.8 7.2 fusion.397
  208.9 32.4 %dynamic_update_slice.294 = f32[2,256,24,64]{1,0,3,2:T(2,128)} dynamic-update-slice(f32[2,256,24,64]{1,0,3,2:T(2,128)} %get-tuple-element.3271, f32[1,256,24,64]{1,0,3,2:T(1,128)} %copy.458, s32[]{:T(128)S(6)} %copy.510, s32[]{:T(128)} %constant.322.clone.1..sunk.3, s32[]{:T(128)} %constant.322.clone.1..sunk.3, s32[]{:T(128)} %constant.322.clone.1..sunk.3) | dynamic-update-slice | bytes 3145732 | tf_op jit(solution)/shard_map/jvp()/while/body/jit(dynamic_update_index_in_dim)/dynamic_update_slice | solution.py:150
  243.5 8.5 multiply_dynamic-update-slice_fusion.3
  263.3 8.0 all-gather.2
  281.9 11.7 all_gather.46
  294.7 9.7 all_gather.48
  305.0 35.2 %while.152 = (s32[]{:T(128)}, f32[512,2,4]{0,2,1:T(4,128)S(1)}, f32[512,2,4]{0,2,1:T(4,128)S(1)}, s32[512]{0:T(512)S(1)}, s32[2,1024]{1,0:T(2,128)S(1)}, /*index...) while((s32[]{:T(128)}, f32[512,2,4]{0,2,1:T(4,128)S(1)}, ...), condition=%wide.region_6.7_spmd.clone, body=%wide.region_3.6_spmd.clone.sunk | while | flops 567824896 | bytes 36157576 | solution.py:203
  305.9 7.4 fusion.386
  313.3 9.3 exponential_reduce_fusion.2
  323.6 7.3 fusion.386
  330.9 9.2 exponential_reduce_fusion.2
  340.2 15.2 %while.153 = (s32[]{:T(128)}, f32[512,2,4,64]{0,3,2,1:T(8,128)S(1)}, bf16[2,1024,2,64]{1,3,2,0:T(8,128)(2,1)}, s32[512]{0:T(512)S(1)}, s32[2,1024]{1,0:T(2,128)S...) while((s32[]{:T(128)}, f32[512,2,4,64]{0,3,2,1:T(8,128)S(1)}, ...), condition=%wide.region_8.9_spmd.clone, body=%wide.region_7.8_spmd.clone.sunk | while | flops 1092616704 | bytes 4243086 | solution.py:219
  341.1 6.7 fusion.392
  348.7 6.7 fusion.392
  359.6 8.2 all-gather.3
  371.8 5.6 reshape.729
  382.5 9.5 multiply_convert_fusion.3
  392.1 5.7 fusion.261
  401.9 36.3 %all-gather.21.cloned.1.call-done = bf16[1024,4096]{1,0:T(8,128)(2,1)} async-done(((bf16[128,4096]{1,0:T(8,128)(2,1)}), bf16[1024,4096]{1,0:T(8,128)(2,1)}) %all-gather.21.cloned.1.call-update) | async-done | bytes 8388624 | tf_op jit(solution)/shard_map/all_gather | solution.py:300
  438.2 12.0 fusion.246
  450.2 35.3 %all-gather.23.cloned.1.call-done = bf16[2048,1024]{1,0:T(8,128)(2,1)} async-done(((bf16[256,1024]{1,0:T(8,128)(2,1)}), bf16[2048,1024]{1,0:T(8,128)(2,1)}) %all-gather.23.cloned.1.call-update) | async-done | bytes 4194320 | tf_op jit(solution)/shard_map/all_gather | solution.py:303
  485.5 9.4 multiply_convert_fusion.1
  494.9 8.1 multiply_reduce_fusion.2
  505.7 6.0 multiply_reduce_fusion
  524.6 61.9 %while.157 = (s32[]{:T(128)}, f32[512,2,4,64]{0,3,2,1:T(8,128)S(1)}, bf16[2,1024,2,64]{1,3,2,0:T(8,128)(2,1)}, bf16[2,1024,2,64]{1,3,2,0:T(8,128)(2,1)}, bf16[2,...) while((s32[]{:T(128)}, f32[512,2,4,64]{0,3,2,1:T(8,128)S(1)}, ...), condition=%wide.region_38.39_spmd.clone, body=%wide.region_37.38_spmd.clone.sunk | while | flops 2728788480 | bytes 190200176 | solution.py:265
  528.2 9.4 fusion.411
  537.7 5.5 fusion.412
  547.2 8.7 fusion.414
  559.1 9.4 fusion.411
  568.5 5.2 fusion.412
  577.8 8.7 fusion.414
  589.4 5.2 reshape.737
  594.6 5.4 reshape.736
  617.8 213.0 %while.151 = (s32[]{:T(128)}, f32[24,64,128]{2,1,0:T(8,128)S(1)}, f32[2,256,24,64]{1,0,3,2:T(2,128)}, bf16[2,256,128]{2,1,0:T(8,128)(2,1)}, f32[2,256,128]{2,1,0...) while((s32[]{:T(128)}, f32[24,64,128]{2,1,0:T(8,128)S(1)}, ...), condition=%wide.region_31.32_spmd, body=%wide.region_21.31_spmd.sunk | while | flops 5051707392 | bytes 175259632 | solution.py:150
  644.7 5.6 fusion.376
  656.2 32.2 %dynamic_update_slice.279 = f32[2,256,24,64]{1,0,3,2:T(2,128)} dynamic-update-slice(f32[2,256,24,64]{1,0,3,2:T(2,128)} %get-tuple-element.3487, f32[1,256,24,64]{1,0,3,2:T(1,128)S(1)} %copy.450, s32[]{:T(128)S(6)} %sub.337, s32[]{:T(128)} %constant.322.clone.1..sunk, s32[]{:T(128)} %constant.322.clone.1..sunk, s32[]{:T(128)} %constant.322.clone.1..sunk) | dynamic-update-slice | bytes 3145732 | tf_op jit(solution)/shard_map/transpose(jvp())/while/body/jit(dynamic_update_index_in_dim)/dynamic_update_slice | solution.py:150
  688.5 10.1 constant_dynamic-slice_fusion.25
  700.4 17.7 %fusion.379 = (f32[256,24]{0,1:T(8,128)}, f32[256,24]{0,1:T(8,128)}, f32[256,256]{1,0:T(8,128)S(1)}) fusion(f32[1,256,256,24]{2,3,1,0:T(8,128)} %get-tuple-element.3120, f32[256,256]{1,0:T(8,128)S(1)} %dynamic-slice_bitcast_fusion.13, pred[1,256,256,24]{2,3,1,0:T(8,128)(4,1)S(1)} %constant_dynamic-slice_fusion.26, ...), kind=kOutput, calls=%fused_computation.258.clone.1 | convolution fusion | flops 1220464640 | bytes 17875968 | tf_op jit(solution)/shard_map/transpose(jvp())/while/body/eval_jaxpr/tsh,shp->thp/dot_general | solution.py:129
  737.7 5.6 fusion.376
  749.3 32.2 %dynamic_update_slice.279 = f32[2,256,24,64]{1,0,3,2:T(2,128)} dynamic-update-slice(f32[2,256,24,64]{1,0,3,2:T(2,128)} %get-tuple-element.3487, f32[1,256,24,64]{1,0,3,2:T(1,128)S(1)} %copy.450, s32[]{:T(128)S(6)} %sub.337, s32[]{:T(128)} %constant.322.clone.1..sunk, s32[]{:T(128)} %constant.322.clone.1..sunk, s32[]{:T(128)} %constant.322.clone.1..sunk) | dynamic-update-slice | bytes 3145732 | tf_op jit(solution)/shard_map/transpose(jvp())/while/body/jit(dynamic_update_index_in_dim)/dynamic_update_slice | solution.py:150
  781.5 10.1 constant_dynamic-slice_fusion.25
  793.5 17.7 %fusion.379 = (f32[256,24]{0,1:T(8,128)}, f32[256,24]{0,1:T(8,128)}, f32[256,256]{1,0:T(8,128)S(1)}) fusion(f32[1,256,256,24]{2,3,1,0:T(8,128)} %get-tuple-element.3120, f32[256,256]{1,0:T(8,128)S(1)} %dynamic-slice_bitcast_fusion.13, pred[1,256,256,24]{2,3,1,0:T(8,128)(4,1)S(1)} %constant_dynamic-slice_fusion.26, ...), kind=kOutput, calls=%fused_computation.258.clone.1 | convolution fusion | flops 1220464640 | bytes 17875968 | tf_op jit(solution)/shard_map/transpose(jvp())/while/body/eval_jaxpr/tsh,shp->thp/dot_general | solution.py:129
  841.3 5.5 fusion.212
  852.0 7.9 convolution_convert_fusion.1
  859.9 9.6 copy.312
  891.1 9.2 convolution_convert_fusion
  902.4 43.2 %reduce-scatter.25.cloned.1.call-done = bf16[128,3352]{1,0:T(8,128)(2,1)} async-done(((bf16[1024,3352]{1,0:T(8,128)(2,1)}), bf16[128,3352]{1,0:T(8,128)(2,1)}) %reduce-scatter.25.cloned.1.call-update) | async-done | bytes 858128
  947.8 31.3 %reduce-scatter.17.cloned.1.call-done = bf16[64,1024]{1,0:T(8,128)(2,1)} async-done(((bf16[512,1024]{1,0:T(8,128)(2,1)}), bf16[64,1024]{1,0:T(8,128)(2,1)}) %reduce-scatter.17.cloned.1.call-update) | async-done | bytes 131088 | tf_op jit(solution)/shard_map/reduce_scatter | solution.py:488
  979.1 35.2 %reduce-scatter.15.cloned.1.call-done = bf16[128,768]{1,0:T(8,128)(2,1)} async-done(((bf16[1024,768]{1,0:T(8,128)(2,1)}), bf16[128,768]{1,0:T(8,128)(2,1)}) %reduce-scatter.15.cloned.1.call-update) | async-done | bytes 196624 | tf_op jit(solution)/shard_map/reduce_scatter | solution.py:485
  1014.3 40.6 %reduce-scatter.19.cloned.1.call-done = bf16[192,1024]{1,0:T(8,128)(2,1)} async-done(((bf16[1536,1024]{1,0:T(8,128)(2,1)}), bf16[192,1024]{1,0:T(8,128)(2,1)}) %reduce-scatter.19.cloned.1.call-update) | async-done | bytes 393232 | tf_op jit(solution)/shard_map/reduce_scatter | solution.py:491
  1054.9 51.2 %reduce-scatter.23.cloned.1.call-done = bf16[256,1024]{1,0:T(8,128)(2,1)} async-done(((bf16[2048,1024]{1,0:T(8,128)(2,1)}), bf16[256,1024]{1,0:T(8,128)(2,1)}) %reduce-scatter.23.cloned.1.call-update) | async-done | bytes 524304 | tf_op jit(solution)/shard_map/reduce_scatter | solution.py:497
  1106.1 89.9 %reduce-scatter.21.cloned.1.call-done = bf16[128,4096]{1,0:T(8,128)(2,1)} async-done(((bf16[1024,4096]{1,0:T(8,128)(2,1)}), bf16[128,4096]{1,0:T(8,128)(2,1)}) %reduce-scatter.21.cloned.1.call-update) | async-done | bytes 1048592 | tf_op jit(solution)/shard_map/reduce_scatter | solution.py:494
  1196.0 6.1 add_convert_fusion.1
  1202.2 38.4 %all-reduce.5 = (f32[24]{0:T(128)}, f32[24]{0:T(128)}, f32[24]{0:T(128)}) all-reduce(f32[24]{0:T(128)S(1)} %get-tuple-element.2453, f32[24]{0:T(128)S(1)} %exponential_multiply_fusion.2, f32[24]{0:T(128)S(1)} %reduce_sum.293), channel_id=1, replica_groups=mesh['fsdp'=8,'ctx'=4] {'fsdp','ctx'}, use_global_device_ids=true, to_apply=%region_61.62 | all-reduce | flops 72 | bytes 576 | tf_op jit(solution)/shard_map/psum | solution.py:517
  1240.6 7.5 fusion.262
  1250.8 15.3 %all-reduce.6 = (bf16[1024]{0:T(1024)(128)(2,1)S(1)}, bf16[1024]{0:T(1024)(128)(2,1)S(1)}) all-reduce(bf16[1024]{0:T(1024)(128)(2,1)S(1)} %get-tuple-element.2223, bf16[1024]{0:T(1024)(128)(2,1)S(1)} %copy-done.139), channel_id=6, replica_groups=mesh['fsdp'=8,'ctx'=4] {'fsdp'}, use_global_device_ids=true, to_apply=%region_43.44.clone | all-reduce | flops 2048 | bytes 8192
  1266.3 9.1 all-reduce.7
  1280.6 7.7 all-reduce.11.cloned.1.call-done
  (749 shorter events, 284.3 us)
Async XLA Ops:
  7.2 75.1 %all-gather.17.cloned.1.call-start = ((), (), s32[]{:S(2)}) async-start(), calls=%async_computation.10 | async-start | bytes 7723008 | tf_op jit(solution)/shard_map/all_gather | solution.py:298
  7.9 269.1 %all-gather.13.cloned.1.call-start = ((), (), s32[]{:S(2)}) async-start(), calls=%async_computation.8 | async-start | bytes 1769472 | tf_op jit(solution)/shard_map/all_gather | solution.py:299
  8.7 368.9 %all-gather.25.cloned.1.call-start = ((), (), s32[]{:S(2)}) async-start(), calls=%async_computation.21 | async-start | bytes 1966080 | tf_op jit(solution)/shard_map/all_gather | solution.py:23
  10.4 78.4 %copy-start.129 = (f32[512]{0:T(512)}, f32[512]{0:T(512)S(1)}, u32[]{:S(2)}) copy-start(f32[512]{0:T(512)S(1)} %add_rsqrt_fusion.1) | copy-start | bytes 6148
  11.1 79.5 %copy-start.137 = (f32[24]{0:T(128)}, f32[24]{0:T(128)S(1)}, u32[]{:S(2)}) copy-start(f32[24]{0:T(128)S(1)} %exp.93) | copy-start | bytes 292
  111.8 9.3 copy-start.19
  111.9 10.6 copy-start.11
  187.1 10.4 copy-start.19
  187.1 10.4 copy-start.51
  187.1 11.7 copy-start.11
  256.3 23.7 %copy-start.5 = (f32[2,256,24,64]{1,3,2,0:T(8,128)}, f32[2,256,24,64]{1,3,2,0:T(8,128)S(1)}, u32[]{:S(2)}) copy-start(f32[2,256,24,64]{1,3,2,0:T(8,128)S(1)} %get-tuple-element.3629) | copy-start | bytes 9437188
  256.4 23.7 %copy-start.17 = (f32[2,256,128]{2,1,0:T(8,128)}, f32[2,256,128]{2,1,0:T(8,128)S(1)}, u32[]{:S(2)}) copy-start(f32[2,256,128]{2,1,0:T(8,128)S(1)} %get-tuple-element.3669) | copy-start | bytes 786436
  256.4 18.8 %copy-start.133 = (f32[24]{0:T(128)S(1)}, f32[24]{0:T(128)}, u32[]{:S(2)}) copy-start(f32[24]{0:T(128)} %param.40) | copy-start | bytes 292
  259.1 133.0 %all-gather.19.cloned.1.call-start = ((), (), s32[]{:S(2)}) async-start(), calls=%async_computation.11 | async-start | bytes 3538944 | tf_op jit(solution)/shard_map/all_gather | solution.py:302
  259.6 138.2 %all-gather.15.cloned.1.call-start = ((), (), s32[]{:S(2)}) async-start(), calls=%async_computation.9 | async-start | bytes 1179648 | tf_op jit(solution)/shard_map/all_gather | solution.py:301
  260.2 178.0 %all-gather.21.cloned.1.call-start = ((), (), s32[]{:S(2)}) async-start(), calls=%async_computation.12 | async-start | bytes 9437184 | tf_op jit(solution)/shard_map/all_gather | solution.py:300
  260.8 224.7 %all-gather.23.cloned.1.call-start = ((), (), s32[]{:S(2)}) async-start(), calls=%async_computation.13 | async-start | bytes 4718592 | tf_op jit(solution)/shard_map/all_gather | solution.py:303
  261.5 345.6 %all-gather.27.cloned.1.call-start = ((), (), s32[]{:S(2)}) async-start(), calls=%async_computation.22 | async-start | bytes 1966080 | tf_op jit(solution)/shard_map/all_gather | solution.py:46
  277.0 27.7 %copy-start.60 = (f32[512,32]{0,1:T(8,128)}, f32[512,32]{0,1:T(8,128)S(1)}, u32[]{:S(2)}) copy-start(f32[512,32]{0,1:T(8,128)S(1)} %get-tuple-element.2506) | copy-start | bytes 196612
  277.0 27.7 %copy-start.62 = (f32[512,32]{0,1:T(8,128)}, f32[512,32]{0,1:T(8,128)S(1)}, u32[]{:S(2)}) copy-start(f32[512,32]{0,1:T(8,128)S(1)} %get-tuple-element.2507) | copy-start | bytes 196612
  294.6 10.3 copy-start.74
  294.6 10.3 copy-start.81
  294.6 10.3 copy-start.84
  294.6 10.3 copy-start.87
  305.0 35.2 %copy-start.44 = (f32[512,2,4,64]{0,3,2,1:T(8,128)S(1)}, f32[512,2,4,64]{0,3,2,1:T(8,128)}, u32[]{:S(2)}) copy-start(f32[512,2,4,64]{0,3,2,1:T(8,128)} %custom-call.2) | copy-start | bytes 3145732
  340.2 17.7 %copy-start.99 = (f32[512,24]{0,1:T(8,128)S(1)}, f32[512,24]{0,1:T(8,128)}, u32[]{:S(2)}) copy-start(f32[512,24]{0,1:T(8,128)} %copy-done.98) | copy-start | bytes 147460
  357.8 14.0 %copy-start.45 = (f32[512,2,4,64]{0,3,2,1:T(8,128)}, f32[512,2,4,64]{0,3,2,1:T(8,128)S(1)}, u32[]{:S(2)}) copy-start(f32[512,2,4,64]{0,3,2,1:T(8,128)S(1)} %get-tuple-element.1497) | copy-start | bytes 3145732
  357.9 39.9 %copy-start.56 = (bf16[512,2,4,64]{0,3,2,1:T(8,128)(2,1)}, bf16[512,2,4,64]{0,3,2,1:T(8,128)(2,1)S(1)}, u32[]{:S(2)}) copy-start(bf16[512,2,4,64]{0,3,2,1:T(8,128)(2,1)S(1)} %convert_element_type.282) | copy-start | bytes 1572868
  359.1 18.3 %copy-start.65 = (f32[24,4,128]{2,0,1:T(8,128)}, f32[24,4,128]{2,0,1:T(8,128)S(1)}, u32[]{:S(2)}) copy-start(f32[24,4,128]{2,0,1:T(8,128)S(1)} %reduce-window.73) | copy-start | bytes 147460
  359.3 18.1 %copy-start.114 = (f32[24,4]{0,1:T(4,128)}, f32[24,4]{0,1:T(4,128)S(1)}, u32[]{:S(2)}) copy-start(f32[24,4]{0,1:T(4,128)S(1)} %slice.156) | copy-start | bytes 1156
  359.4 12.4 copy-start.112
  377.5 137.9 %copy-start.71 = (f32[512,24]{0,1:T(8,128)}, f32[512,24]{0,1:T(8,128)S(1)}, u32[]{:S(2)}) copy-start(f32[512,24]{0,1:T(8,128)S(1)} %exponential_multiply_fusion.1) | copy-start | bytes 147460
  382.5 9.6 copy-start.8
  382.5 9.5 copy-start.140
  397.8 40.4 %copy-start.122 = (f32[1024]{0:T(1024)S(1)}, f32[1024]{0:T(1024)}, u32[]{:S(2)}) copy-start(f32[1024]{0:T(1024)} %param.31) | copy-start | bytes 12292
  401.9 101.1 %copy-start.116 = (f32[512]{0:T(512)}, f32[512]{0:T(512)S(1)}, u32[]{:S(2)}) copy-start(f32[512]{0:T(512)S(1)} %add_rsqrt_fusion) | copy-start | bytes 6148
  438.2 47.3 %copy-start.46 = (bf16[512,1024]{1,0:T(8,128)(2,1)S(1)}, bf16[512,1024]{1,0:T(8,128)(2,1)}, u32[]{:S(2)}) copy-start(bf16[512,1024]{1,0:T(8,128)(2,1)} %param.41) | copy-start | bytes 3145732
  485.5 9.4 copy-start.31
  485.5 9.4 copy-start.142
  520.5 353.2 %reduce-scatter.11.cloned.1.call-start = ((), (), s32[]{:S(2)}) async-start(), calls=%async_computation.14 | async-start | bytes 655360 | tf_op jit(solution)/shard_map/reduce_scatter | solution.py:444
  527.3 10.3 copy-start.2
  558.2 10.3 copy-start.2
  588.7 286.2 %reduce-scatter.13.cloned.1.call-start = ((), (), s32[]{:S(2)}) async-start(), calls=%async_computation.15 | async-start | bytes 655360 | tf_op jit(solution)/shard_map/reduce_scatter | solution.py:447
  607.1 338.5 %reduce-scatter.25.cloned.1.call-start = ((), (), s32[]{:S(2)}) async-start(), calls=%async_computation.23 | async-start | bytes 7962624
  688.5 10.1 copy-start.53
  688.5 10.1 copy-start.27
  700.4 17.8 %copy-start.21 = (f32[2,256,128]{2,1,0:T(8,128)S(1)}, f32[2,256,128]{2,1,0:T(8,128)}, u32[]{:S(2)}) copy-start(f32[2,256,128]{2,1,0:T(8,128)} %get-tuple-element.3529) | copy-start | bytes 786436 | tf_op jit(solution)/shard_map/transpose(jvp())/while
  700.4 17.8 %copy-start.95 = (bf16[2,256,128]{2,1,0:T(8,128)(2,1)S(1)}, bf16[2,256,128]{2,1,0:T(8,128)(2,1)}, u32[]{:S(2)}) copy-start(bf16[2,256,128]{2,1,0:T(8,128)(2,1)} %get-tuple-element.3488) | copy-start | bytes 393220 | tf_op jit(solution)/shard_map/transpose(jvp())/while
  700.4 18.5 %copy-start.13 = (f32[2,24,64,128]{3,2,1,0:T(8,128)S(1)}, f32[2,24,64,128]{3,2,1,0:T(8,128)}, u32[]{:S(2)}) copy-start(f32[2,24,64,128]{3,2,1,0:T(8,128)} %get-tuple-element.3666) | copy-start | bytes 4718596 | tf_op jit(solution)/shard_map/transpose(jvp())/while
  700.4 18.5 %copy-start.43 = (f32[256,24]{0,1:T(8,128)S(1)}, f32[256,24]{0,1:T(8,128)}, u32[]{:S(2)}) copy-start(f32[256,24]{0,1:T(8,128)} %copy-done.42) | copy-start | bytes 73732 | tf_op jit(solution)/shard_map/transpose(jvp())/while
  781.5 10.1 copy-start.53
  781.5 10.1 copy-start.27
  793.5 17.8 %copy-start.21 = (f32[2,256,128]{2,1,0:T(8,128)S(1)}, f32[2,256,128]{2,1,0:T(8,128)}, u32[]{:S(2)}) copy-start(f32[2,256,128]{2,1,0:T(8,128)} %get-tuple-element.3529) | copy-start | bytes 786436 | tf_op jit(solution)/shard_map/transpose(jvp())/while
  793.5 17.8 %copy-start.95 = (bf16[2,256,128]{2,1,0:T(8,128)(2,1)S(1)}, bf16[2,256,128]{2,1,0:T(8,128)(2,1)}, u32[]{:S(2)}) copy-start(bf16[2,256,128]{2,1,0:T(8,128)(2,1)} %get-tuple-element.3488) | copy-start | bytes 393220 | tf_op jit(solution)/shard_map/transpose(jvp())/while
  793.5 18.5 %copy-start.13 = (f32[2,24,64,128]{3,2,1,0:T(8,128)S(1)}, f32[2,24,64,128]{3,2,1,0:T(8,128)}, u32[]{:S(2)}) copy-start(f32[2,24,64,128]{3,2,1,0:T(8,128)} %get-tuple-element.3666) | copy-start | bytes 4718596 | tf_op jit(solution)/shard_map/transpose(jvp())/while
  793.5 18.5 %copy-start.43 = (f32[256,24]{0,1:T(8,128)S(1)}, f32[256,24]{0,1:T(8,128)}, u32[]{:S(2)}) copy-start(f32[256,24]{0,1:T(8,128)} %copy-done.42) | copy-start | bytes 73732 | tf_op jit(solution)/shard_map/transpose(jvp())/while
  830.9 10.4 copy-start.113
  869.5 109.6 %reduce-scatter.17.cloned.1.call-start = ((), (), s32[]{:S(2)}) async-start(), calls=%async_computation.17 | async-start | bytes 1179648 | tf_op jit(solution)/shard_map/reduce_scatter | solution.py:488
  873.4 140.9 %reduce-scatter.15.cloned.1.call-start = ((), (), s32[]{:S(2)}) async-start(), calls=%async_computation.16 | async-start | bytes 1769472 | tf_op jit(solution)/shard_map/reduce_scatter | solution.py:485
  878.3 176.6 %reduce-scatter.19.cloned.1.call-start = ((), (), s32[]{:S(2)}) async-start(), calls=%async_computation.18 | async-start | bytes 3538944 | tf_op jit(solution)/shard_map/reduce_scatter | solution.py:491
  883.2 222.9 %reduce-scatter.23.cloned.1.call-start = ((), (), s32[]{:S(2)}) async-start(), calls=%async_computation.20 | async-start | bytes 4718592 | tf_op jit(solution)/shard_map/reduce_scatter | solution.py:497
  889.5 306.5 %reduce-scatter.21.cloned.1.call-start = ((), (), s32[]{:S(2)}) async-start(), calls=%async_computation.19 | async-start | bytes 9437184 | tf_op jit(solution)/shard_map/reduce_scatter | solution.py:494
  900.3 387.9 %all-reduce.11.cloned.1.call-start = ((), (), s32[]{:S(2)}) async-start(), calls=%async_computation.24 | async-start | bytes 6303744 | tf_op jit(solution)/shard_map/psum | solution.py:508
  1248.1 28.3 %copy-start.119 = (f32[512]{0:T(512)S(1)}, f32[512]{0:T(512)}, u32[]{:S(2)}) copy-start(f32[512]{0:T(512)} %copy-done.118) | copy-start | bytes 6148
  (156 other events, 645.0 us)
Sparse Core Ops, SparseCore 0:
  9.6 72.5 all-gather.16
  83.9 23.2 all-gather.12
  259.2 31.0 all-gather.24
  291.8 40.7 all-gather.18
  334.0 20.9 all-gather.14
  356.5 81.7 all-gather.20
  439.8 45.6 all-gather.22
  520.6 29.6 all-gather.26
  588.8 23.5 reduce-scatter.10
  615.3 24.7 reduce-scatter.12
  869.6 75.9 reduce-scatter.24
  948.3 30.7 reduce-scatter.16
  982.0 32.2 reduce-scatter.14
  1016.4 38.3 reduce-scatter.18
  1057.0 48.9 reduce-scatter.22
  1108.2 87.7 reduce-scatter.20
  1200.2 87.9 all-reduce.10
where the time goes:
time: 1320 us; the launch traced here: 1300 us
  waiting for transfers between devices  444 us (34%)
  matrix products  308 us (23%)
  local copies, waits for them, and re-layouts  279 us (21%)
  other arithmetic  123 us (9%)
  blocking collectives  100 us (8%)
  loops' own time  30.8 us (2%)
  between operations  17.5 us (1%)
    dynamic_update_slice x22, local copies, waits for them, and re-layouts, ssd_blocks(): (state, last), results = lax.scan(step, init, items)  148 us
    reduce_scatter x1, waiting for transfers between devices, shards(): lax.psum_scatter(gradients[4].astype(jnp.bfloat16), 'fsdp', scatter_dimen...  89.9 us
    all_gather x1, waiting for transfers between devices, shards(): lax.all_gather(w_in, 'fsdp', axis=0, tiled=True)  69.9 us
    dot_general x6, matrix products, step(): result = jnp.einsum('tsh,shp->thp', mixing, scaled, precision=HIGH)  61 us
    reduce_scatter x1, waiting for transfers between devices, shards(): lax.psum_scatter(gradients[5].astype(jnp.bfloat16), 'fsdp', scatter_dimen...  51.2 us
    unnamed x18, waiting for transfers between devices  47.1 us
    reduce_scatter x1, waiting for transfers between devices, shards(): lax.psum_scatter(gradients[3].astype(jnp.bfloat16), 'fsdp', scatter_dimen...  40.6 us
    psum x1, blocking collectives, shards(): lax.psum((dt_bias_grad, a_log_grad, d_skip_grad), ('fsdp', 'ctx'))  38.4 us
  transfers between devices with their start and end apart: 17, of which 10 were waited for; matrix products, arithmetic and copies ran while one was open for 49% of the time, Pallas kernels for 0%

commit v1 on v0

v1 whole, which is shorter than its diff:
```python
import functools

import jax
import jax.numpy as jnp
from jax import lax
from jax.experimental import pallas as pl
from jax.experimental.pallas import tpu as pltpu
from jax.sharding import PartitionSpec as P

FF = 2048
QUERY_HEADS = 8
KEY_VALUE_HEADS = 2
HEAD_WIDTH = 64
MH = 24
PD = 64
ST = 128
D_SSM = MH * PD
PAIRS = MH // 2
LANES = 128

EPS = 1e-05
ROPE_BASE = 100000000000.0
HIGH = lax.Precision.HIGHEST
F32 = jnp.float32
BF16 = jnp.bfloat16

NN = ((1,), (0,))
NT = ((1,), (1,))
TN = ((0,), (0,))
FLOW_ROWS = 16
VMEM_LIMIT = 56 * 1024 * 1024


def mm(left, right, dims=NN, precision=None):
    return lax.dot_general(
        left, right, (dims, ((), ())), precision=precision, preferred_element_type=F32
    )


def params(*semantics):
    return pltpu.CompilerParams(
        dimension_semantics=semantics or None, vmem_limit_bytes=VMEM_LIMIT
    )


def behind(kernel, inputs, extra):
    if not extra:
        return kernel

    def run(*refs):
        kernel(*refs[:inputs], *refs[inputs + extra :])

    return run


def anywhere(count):
    return [pl.BlockSpec(memory_space=pl.ANY)] * count


def smem():
    return pl.BlockSpec(memory_space=pltpu.SMEM)


def whole():
    return pl.BlockSpec(memory_space=pltpu.VMEM)


def swap_halves(block):
    half = HEAD_WIDTH // 2
    lane = lax.broadcasted_iota(jnp.int32, block.shape, 1)
    ahead = pltpu.roll(block, LANES - half, 1)
    behind = pltpu.roll(block, half, 1)
    return jnp.where(lax.rem(lane, HEAD_WIDTH) < half, ahead, behind)


def rotate_kernel(qkv_ref, cos_ref, sin_ref, q_ref, kv_ref):
    cos, sin = cos_ref[...], sin_ref[...]
    q_cols = QUERY_HEADS * HEAD_WIDTH
    for start in range(0, q_cols, LANES):
        block = qkv_ref[:, start : start + LANES]
        turned = (block * cos + swap_halves(block) * sin).astype(BF16)
        q_ref[:, start : start + LANES] = turned * jnp.asarray(HEAD_WIDTH**-0.5, BF16)
    block = qkv_ref[:, q_cols : q_cols + LANES]
    keys = block * cos + swap_halves(block) * sin
    values = qkv_ref[:, q_cols + LANES :]
    lane = lax.broadcasted_iota(jnp.int32, keys.shape, 1)
    first = lane < HEAD_WIDTH
    kv_ref[0] = jnp.where(first, keys, pltpu.roll(values, HEAD_WIDTH, 1)).astype(BF16)
    kv_ref[1] = jnp.where(first, pltpu.roll(keys, HEAD_WIDTH, 1), values).astype(BF16)


def rotate(qkv, cos, sin):
    rows = qkv.shape[0]
    return pl.pallas_call(
        rotate_kernel,
        out_shape=(
            jax.ShapeDtypeStruct((rows, QUERY_HEADS * HEAD_WIDTH), BF16),
            jax.ShapeDtypeStruct((KEY_VALUE_HEADS, rows, LANES), BF16),
        ),
        in_specs=[whole()] * 3,
        out_specs=(whole(), whole()),
        compiler_params=params(),
        name="rotate",
    )(qkv, cos, sin)


def unrotate_kernel(dq_ref, dkv_ref, cos_ref, sin_ref, out_ref):
    cos, sin = cos_ref[...], sin_ref[...]
    q_cols = QUERY_HEADS * HEAD_WIDTH
    for start in range(0, q_cols, LANES):
        block = dq_ref[:, start : start + LANES]
        out_ref[:, start : start + LANES] = (block * cos - swap_halves(block) * sin).astype(BF16)
    zero = dkv_ref[0].astype(F32)
    one = dkv_ref[1].astype(F32)
    lane = lax.broadcasted_iota(jnp.int32, zero.shape, 1)
    first = lane < HEAD_WIDTH
    keys = jnp.where(first, zero, pltpu.roll(one, HEAD_WIDTH, 1))
    values = jnp.where(first, pltpu.roll(zero, HEAD_WIDTH, 1), one)
    out_ref[:, q_cols : q_cols + LANES] = (keys * cos - swap_halves(keys) * sin).astype(BF16)
    out_ref[:, q_cols + LANES :] = values.astype(BF16)


def unrotate(dq, dkv, cos, sin):
    rows = dq.shape[0]
    return pl.pallas_call(
        unrotate_kernel,
        out_shape=jax.ShapeDtypeStruct((rows, dq.shape[1] + 2 * LANES), BF16),
        in_specs=[whole()] * 4,
        out_specs=whole(),
        compiler_params=params(),
        name="unrotate",
    )(dq, dkv, cos, sin)


def visible(key_block, place, rows, start):
    key_index = key_block * rows + lax.broadcasted_iota(jnp.int32, (rows, rows), 0)
    query_index = place * rows + lax.broadcasted_iota(jnp.int32, (1, rows), 1)
    return (key_index >= start) & (key_index <= query_index)


def attend_kernel(place_ref, q_ref, kv_ref, start_ref, o_ref, lse_ref, top_s, mass_s, acc_s):
    rows = q_ref.shape[0]
    place = place_ref[0]
    share = QUERY_HEADS // KEY_VALUE_HEADS
    top_s[...] = jnp.full(top_s.shape, -1e30, F32)
    mass_s[...] = jnp.zeros(mass_s.shape, F32)
    acc_s[...] = jnp.zeros(acc_s.shape, F32)
    start = start_ref[...]

    def block(back, unused):
        keys = kv_ref[back, 0, :, :HEAD_WIDTH]
        values = kv_ref[back, 0, :, HEAD_WIDTH:]
        seen = visible(place - back, place, rows, start)
        for r in range(share):
            queries = q_ref[:, r * HEAD_WIDTH : (r + 1) * HEAD_WIDTH]
            scores = jnp.where(seen, mm(keys, queries, NT), -1e30)
            old = top_s[r : r + 1, :]
            new = jnp.maximum(old, jnp.max(scores, axis=0, keepdims=True))
            probs = jnp.exp(scores - new)
            scale = jnp.exp(old - new)
            top_s[r : r + 1, :] = new
            mass_s[r : r + 1, :] = mass_s[r : r + 1, :] * scale + jnp.sum(
                probs, axis=0, keepdims=True
            )
            at = slice(r * HEAD_WIDTH, (r + 1) * HEAD_WIDTH)
            acc_s[at, :] = acc_s[at, :] * scale + mm(values, probs.astype(BF16), TN)
        return unused

    lax.fori_loop(0, place + 1, block, 0)
    lse_ref[0] = top_s[...] + jnp.log(mass_s[...])
    for r in range(share):
        at = slice(r * HEAD_WIDTH, (r + 1) * HEAD_WIDTH)
        acc_s[at, :] = acc_s[at, :] / mass_s[r : r + 1, :]
    o_ref[...] = jnp.transpose(acc_s[...])


def attend(place, q, kv_all, start):
    rows = q.shape[0]
    blocks = kv_all.shape[0]
    share = QUERY_HEADS // KEY_VALUE_HEADS
    wide = share * HEAD_WIDTH
    return pl.pallas_call(
        attend_kernel,
        grid=(KEY_VALUE_HEADS,),
        out_shape=(
            jax.ShapeDtypeStruct(q.shape, F32),
            jax.ShapeDtypeStruct((KEY_VALUE_HEADS, share, rows), F32),
        ),
        in_specs=[
            smem(),
            pl.BlockSpec((rows, wide), lambda g: (0, g)),
            pl.BlockSpec((blocks, 1, rows, LANES), lambda g: (0, g, 0, 0)),
            pl.BlockSpec((1, rows), lambda g: (0, 0)),
        ],
        out_specs=(
            pl.BlockSpec((rows, wide), lambda g: (0, g)),
            pl.BlockSpec((1, share, rows), lambda g: (g, 0, 0)),
        ),
        scratch_shapes=[
            pltpu.VMEM((share, rows), F32),
            pltpu.VMEM((share, rows), F32),
            pltpu.VMEM((wide, rows), F32),
        ],
        compiler_params=params("arbitrary"),
        name="attend",
    )(place, q, kv_all, start)


def attend_back_kernel(
    place_ref, q_ref, kv_ref, start_ref, lse_ref, o_ref, do_ref, dq_ref, dkv_ref, delta_s, dq_s
):
    rows = q_ref.shape[0]
    place = place_ref[0]
    share = QUERY_HEADS // KEY_VALUE_HEADS
    back = pl.program_id(1)

    @pl.when(back == 0)
    def begin():
        flat = jnp.transpose(do_ref[...].astype(F32) * o_ref[...])
        for r in range(share):
            at = slice(r * HEAD_WIDTH, (r + 1) * HEAD_WIDTH)
            delta_s[r : r + 1, :] = jnp.sum(flat[at, :], axis=0, keepdims=True)
        dq_s[...] = jnp.zeros(dq_s.shape, F32)

    @pl.when(back <= place)
    def work():
        keys = kv_ref[0, 0, :, :HEAD_WIDTH]
        values = kv_ref[0, 0, :, HEAD_WIDTH:]
        seen = visible(place - back, place, rows, start_ref[...])
        d_keys = jnp.zeros((rows, HEAD_WIDTH), F32)
        d_values = jnp.zeros((rows, HEAD_WIDTH), F32)
        for r in range(share):
            at = slice(r * HEAD_WIDTH, (r + 1) * HEAD_WIDTH)
            queries = q_ref[:, at]
            d_out = do_ref[:, at]
            scores = mm(keys, queries, NT)
            probs = jnp.where(seen, jnp.exp(scores - lse_ref[0, r : r + 1, :]), 0.0)
            d_values = d_values + mm(probs.astype(BF16), d_out)
            d_probs = mm(values, d_out, NT)
            d_scores = (probs * (d_probs - delta_s[r : r + 1, :])).astype(BF16)
            d_keys = d_keys + mm(d_scores, queries)
            dq_s[at, :] = dq_s[at, :] + mm(keys, d_scores, TN)
        dkv_ref[0, 0] = jnp.concatenate([d_keys, d_values], axis=1).astype(BF16)

    @pl.when(back > place)
    def nothing():
        dkv_ref[0, 0] = jnp.zeros((rows, LANES), BF16)

    @pl.when(back == pl.num_programs(1) - 1)
    def end():
        dq_ref[...] = jnp.transpose(dq_s[...]) * HEAD_WIDTH**-0.5


def attend_back(place, q, kv_all, start, lse, o, d_o, after=()):
    rows = q.shape[0]
    blocks = kv_all.shape[0]
    share = QUERY_HEADS // KEY_VALUE_HEADS
    wide = share * HEAD_WIDTH
    side = pl.BlockSpec((rows, wide), lambda g, j: (0, g))
    block = pl.BlockSpec((1, 1, rows, LANES), lambda g, j: (j, g, 0, 0))
    return pl.pallas_call(
        behind(attend_back_kernel, 7, len(after)),
        grid=(KEY_VALUE_HEADS, blocks),
        out_shape=(
            jax.ShapeDtypeStruct(q.shape, F32),
            jax.ShapeDtypeStruct(kv_all.shape, BF16),
        ),
        in_specs=[
            smem(),
            side,
            block,
            pl.BlockSpec((1, rows), lambda g, j: (0, 0)),
            pl.BlockSpec((1, share, rows), lambda g, j: (g, 0, 0)),
            side,
            side,
        ]
        + anywhere(len(after)),
        out_specs=(side, block),
        scratch_shapes=[pltpu.VMEM((share, rows), F32), pltpu.VMEM((wide, rows), F32)],
        compiler_params=params("arbitrary", "arbitrary"),
        name="attend_back",
    )(place, q, kv_all, start, lse, o, d_o, *after)


LANE_DT, LANE_CUM, LANE_KEEP, LANE_TAIL = 0, 32, 64, 96


def chunk_of(rows):
    return min(256, rows)


def triangle(size, lower):
    row = lax.broadcasted_iota(jnp.int32, (size, size), 0)
    col = lax.broadcasted_iota(jnp.int32, (size, size), 1)
    return (row >= col if lower else row <= col).astype(F32)


def pair_wide(pack, lane):
    rows = pack.shape[0]
    at = lax.broadcasted_iota(jnp.int32, (rows, LANES), 1)
    return jnp.where(at < PD, pack[:, lane : lane + 1], pack[:, lane + 1 : lane + 2])


def softplus(value):
    return jnp.maximum(value, 0.0) + jnp.log1p(jnp.exp(-jnp.abs(value)))


def flow_rows(flow):
    row = lax.broadcasted_iota(jnp.int32, (FLOW_ROWS, flow.shape[1]), 0)
    high = flow.astype(BF16).astype(F32)
    middle = (flow - high).astype(BF16).astype(F32)
    low = flow - high - middle
    parts = jnp.where(row == 0, high, jnp.where(row == 1, middle, jnp.where(row == 2, low, 0.0)))
    return parts.astype(BF16)


def ssm_state_kernel(
    prev_ref, dtr_ref, bias_ref, alog_ref, seg_ref, x_ref, b_ref, pack_ref, flip_ref, far_ref,
    state_ref,
):
    rows = dtr_ref.shape[0]
    span = chunk_of(rows)
    count = rows // span
    dt = softplus(dtr_ref[...] + bias_ref[...])
    logd = -dt * jnp.exp(alog_ref[...])
    lower = triangle(span, True)
    gap = jnp.zeros((span, 32 - MH), F32)
    keeps, tails = [], []
    for c in range(count):
        at = slice(c * span, (c + 1) * span)
        cum = mm(lower, logd[at], precision=HIGH)
        seg = seg_ref[at, :]
        before = prev_ref[0] if c == 0 else seg_ref[c * span - 1 : c * span, :]
        keep = jnp.where(seg == before, jnp.exp(cum), 0.0)
        tail = jnp.where(seg == seg[span - 1 : span, :], jnp.exp(cum[span - 1 : span] - cum), 0.0)
        pack = jnp.concatenate([dt[at], gap, cum, gap, keep, gap, tail, gap], axis=1)
        pack_ref[at, :] = pack
        flip_ref[:, at] = jnp.transpose(pack)
        keeps.append(keep)
        tails.append(tail)
    flow = jnp.ones((1, MH), F32)
    far = []
    for c in range(count):
        far.append(keeps[c] * flow)
        flow = flow * keeps[c][span - 1 : span]
    far_ref[...] = jnp.concatenate(
        [jnp.concatenate(far, axis=0), jnp.zeros((rows, LANES - MH), F32)], axis=1
    )
    after = jnp.ones((1, MH), F32)
    weights = [None] * count
    for c in reversed(range(count)):
        weights[c] = tails[c] * dt[c * span : (c + 1) * span] * after
        after = after * keeps[c][span - 1 : span]
    weight = jnp.concatenate(weights, axis=0)
    b_vals = b_ref[...]
    for j in range(PAIRS):
        at = slice(j * LANES, (j + 1) * LANES)
        scaled = (x_ref[:, at].astype(F32) * pair_wide(weight, 2 * j)).astype(BF16)
        state_ref[:ST, at] = mm(b_vals, scaled, TN).astype(BF16)
        state_ref[ST:, at] = flow_rows(pair_wide(flow, 2 * j))


def ssm_state(prev, dt_raw, bias, a_log, seg_col, x, b_vals):
    rows = dt_raw.shape[0]
    return pl.pallas_call(
        ssm_state_kernel,
        out_shape=(
            jax.ShapeDtypeStruct((rows, LANES), F32),
            jax.ShapeDtypeStruct((LANES, rows), F32),
            jax.ShapeDtypeStruct((rows, LANES), F32),
            jax.ShapeDtypeStruct((ST + FLOW_ROWS, D_SSM), BF16),
        ),
        in_specs=[smem()] + [whole()] * 6,
        out_specs=(whole(),) * 4,
        compiler_params=params(),
        name="ssm_state",
    )(prev, dt_raw, bias, a_log, seg_col, x, b_vals)


def same_lower(seg_col, seg_row, span, transposed):
    row = lax.broadcasted_iota(jnp.int32, (span, span), 0)
    col = lax.broadcasted_iota(jnp.int32, (span, span), 1)
    order = row <= col if transposed else row >= col
    return order & (seg_col == seg_row)


def ssm_forward_kernel(
    pack_ref, flip_ref, segc_ref, segr_ref, x_ref, b_ref, c_ref, z_ref, skip_ref, enter_ref,
    gated_ref, y_ref, inner_s,
):
    rows = x_ref.shape[0]
    span = chunk_of(rows)
    count = rows // span
    j = pl.program_id(0)

    @pl.when(j == 0)
    def begin():
        for c in range(count):
            at = slice(c * span, (c + 1) * span)
            mask = same_lower(segc_ref[at, :], segr_ref[:, at], span, False)
            inner_s[c] = jnp.where(mask, mm(c_ref[at, :], b_ref[at, :], NT), 0.0)

    lane = lax.broadcasted_iota(jnp.int32, (span, LANES), 1)
    state = enter_ref[...]
    for c in range(count):
        at = slice(c * span, (c + 1) * span)
        pack = pltpu.roll(pack_ref[at, :], lax.rem(LANES - 2 * j, LANES), 1)
        x = x_ref[at, :].astype(F32)
        scaled = x * pair_wide(pack, LANE_DT)
        scaled_low = scaled.astype(BF16)
        keep = pair_wide(pack, LANE_KEEP)
        mixed = keep * mm(c_ref[at, :], state.astype(BF16))
        parts = []
        for k in range(2):
            column = pack[:, LANE_CUM + k : LANE_CUM + k + 1]
            row = flip_ref[pl.ds(LANE_CUM + 2 * j + k, 1), at]
            mixing = inner_s[c] * jnp.exp(jnp.minimum(column - row, 0.0))
            parts.append(mm(mixing.astype(BF16), scaled_low))
        mixed = mixed + jnp.where(lane < PD, parts[0], parts[1])
        mixed = mixed + skip_ref[:, :] * x
        y_ref[at, :] = mixed
        z = z_ref[at, :]
        gated_ref[at, :] = (mixed * (z * jax.nn.sigmoid(z))).astype(BF16)
        if c + 1 < count:
            tail = pair_wide(pack, LANE_TAIL)
            fresh = mm(b_ref[at, :], (tail * scaled).astype(BF16), TN)
            state = keep[span - 1 : span, :] * state + fresh


def pair_block(rows):
    return pl.BlockSpec((rows, LANES), lambda j: (0, j))


def held(shape):
    return pl.BlockSpec(shape, lambda j: (0,) * len(shape))


def ssm_forward(pack, flip, seg_col, seg_row, x, b_vals, c_vals, z, skip_wide, enter):
    rows = x.shape[0]
    span = chunk_of(rows)
    return pl.pallas_call(
        ssm_forward_kernel,
        grid=(PAIRS,),
        out_shape=(
            jax.ShapeDtypeStruct((rows, D_SSM), BF16),
            jax.ShapeDtypeStruct((rows, D_SSM), F32),
        ),
        in_specs=[
            held(pack.shape),
            held(flip.shape),
            held(seg_col.shape),
            held(seg_row.shape),
            pair_block(rows),
            held(b_vals.shape),
            held(c_vals.shape),
            pair_block(rows),
            pair_block(1),
            pair_block(ST),
        ],
        out_specs=(pair_block(rows), pair_block(rows)),
        scratch_shapes=[pltpu.VMEM((rows // span, span, span), F32)],
        compiler_params=params("arbitrary"),
        name="ssm_forward",
    )(pack, flip, seg_col, seg_row, x, b_vals, c_vals, z, skip_wide, enter)


def ssm_gate_back_kernel(
    far_ref, dg_ref, y_ref, z_ref, c_ref, flow_ref, dz_ref, dy_ref, state_ref
):
    j = pl.program_id(0)
    far = pltpu.roll(far_ref[...], lax.rem(LANES - 2 * j, LANES), 1)
    z = z_ref[...]
    sigmoid = jax.nn.sigmoid(z)
    d_gated = dg_ref[...].astype(F32)
    dy = d_gated * (z * sigmoid)
    dz_ref[...] = (d_gated * y_ref[...] * sigmoid * (1.0 + z * (1.0 - sigmoid))).astype(BF16)
    dy_ref[...] = dy.astype(BF16)
    entered = (pair_wide(far, 0) * dy).astype(BF16)
    state_ref[:ST, :] = mm(c_ref[...], entered, TN).astype(BF16)
    state_ref[ST:, :] = flow_ref[...]


def ssm_gate_back(far, d_gated, y, z, c_vals, flow, after=()):
    rows = y.shape[0]
    return pl.pallas_call(
        behind(ssm_gate_back_kernel, 6, len(after)),
        grid=(PAIRS,),
        out_shape=(
            jax.ShapeDtypeStruct((rows, D_SSM), BF16),
            jax.ShapeDtypeStruct((rows, D_SSM), BF16),
            jax.ShapeDtypeStruct((ST + FLOW_ROWS, D_SSM), BF16),
        ),
        in_specs=[
            held(far.shape),
            pair_block(rows),
            pair_block(rows),
            pair_block(rows),
            held(c_vals.shape),
            pair_block(FLOW_ROWS),
        ]
        + anywhere(len(after)),
        out_specs=(pair_block(rows), pair_block(rows), pair_block(ST + FLOW_ROWS)),
        compiler_params=params("arbitrary"),
        name="ssm_gate_back",
    )(far, d_gated, y, z, c_vals, flow, *after)


def ssm_back_kernel(
    pack_ref, flip_ref, segc_ref, segr_ref, x_ref, dy_ref, b_ref, c_ref, skip_ref, enter_ref,
    leave_ref, dtr_ref, bias_ref, alog_ref, dx_ref, db_ref, dc_ref, ddt_ref, sums_ref,
    inner_s, d_inner_s, col_s, row_s, direct_s, db_s, dc_s, skip_s,
):
    rows = x_ref.shape[0]
    span = chunk_of(rows)
    count = rows // span
    j = pl.program_id(0)
    lane = lax.broadcasted_iota(jnp.int32, (span, LANES), 1)
    first = lane < PD

    @pl.when(j == 0)
    def begin():
        for c in range(count):
            at = slice(c * span, (c + 1) * span)
            mask = same_lower(segc_ref[at, :], segr_ref[:, at], span, True)
            inner_s[c] = jnp.where(mask, mm(b_ref[at, :], c_ref[at, :], NT), 0.0)
        d_inner_s[...] = jnp.zeros(d_inner_s.shape, F32)
        col_s[...] = jnp.zeros(col_s.shape, F32)
        row_s[...] = jnp.zeros(row_s.shape, F32)
        direct_s[...] = jnp.zeros(direct_s.shape, F32)
        db_s[...] = jnp.zeros(db_s.shape, F32)
        dc_s[...] = jnp.zeros(dc_s.shape, F32)
        skip_s[...] = jnp.zeros(skip_s.shape, F32)

    packs = [
        pltpu.roll(pack_ref[c * span : (c + 1) * span, :], lax.rem(LANES - 2 * j, LANES), 1)
        for c in range(count)
    ]
    skip = skip_ref[:, :]
    states = [enter_ref[...]]
    for c in range(count - 1):
        at = slice(c * span, (c + 1) * span)
        last = pair_wide(packs[c], LANE_KEEP)[span - 1 : span, :]
        weight = pair_wide(packs[c], LANE_DT) * pair_wide(packs[c], LANE_TAIL)
        fresh = mm(b_ref[at, :], (weight * x_ref[at, :].astype(F32)).astype(BF16), TN)
        states.append(last * states[c] + fresh)
    later = leave_ref[...]
    for c in reversed(range(count)):
        at = slice(c * span, (c + 1) * span)
        pack, state = packs[c], states[c]
        b_vals, c_vals = b_ref[at, :], c_ref[at, :]
        x = x_ref[at, :].astype(F32)
        dy_low = dy_ref[at, :]
        dy = dy_low.astype(F32)
        dt = pair_wide(pack, LANE_DT)
        keep = pair_wide(pack, LANE_KEEP)
        tail = pair_wide(pack, LANE_TAIL)
        scaled = dt * x
        scaled_low = scaled.astype(BF16)
        state_low, later_low = state.astype(BF16), later.astype(BF16)
        kept_low = (keep * dy).astype(BF16)
        entered = keep * mm(c_vals, state_low)
        d_scaled_later = tail * mm(b_vals, later_low)
        dc_s[at, :] += mm(kept_low, state_low, NT)
        db_s[at, :] += mm((tail * scaled).astype(BF16), later_low, NT)
        parts, squares = [], []
        for k in range(2):
            column = pack[:, LANE_CUM + k : LANE_CUM + k + 1]
            row = flip_ref[pl.ds(LANE_CUM + 2 * j + k, 1), at]
            decay = jnp.exp(jnp.minimum(row - column, 0.0))
            mixing = inner_s[c] * decay
            own = jnp.where(first if k == 0 else ~first, scaled, 0.0).astype(BF16)
            d_mixing = mm(own, dy_low, NT)
            d_inner_s[c] += d_mixing * decay
            parts.append(mm(mixing.astype(BF16), dy_low))
            square = d_mixing * mixing
            squares.append(jnp.sum(square, axis=1, keepdims=True))
            row_s[pl.ds(2 * j + k, 1), at] = jnp.sum(square, axis=0, keepdims=True)
        d_scaled = jnp.where(first, parts[0], parts[1]) + d_scaled_later
        dx_ref[at, :] = (dt * d_scaled + skip * dy).astype(BF16)
        crossing = state * later
        crossing = jnp.sum(crossing, axis=0, keepdims=True) * keep[span - 1 : span, :]
        through = entered * dy
        leaving = scaled * d_scaled_later
        touching = x * d_scaled
        skipped = jnp.sum(dy * x, axis=0, keepdims=True)
        at_end = lax.broadcasted_iota(jnp.int32, (span, 1), 0) == span - 1
        for k in range(2):
            own = first if k == 0 else ~first
            own_row = own[:1, :]

            def side(value):
                return jnp.sum(jnp.where(own, value, 0.0), axis=1, keepdims=True)

            def side_row(value):
                return jnp.sum(jnp.where(own_row, value, 0.0), axis=1, keepdims=True)

            left = side(leaving)
            column = side(through) - left - squares[k]
            ending = jnp.sum(left, axis=0, keepdims=True) + side_row(crossing)
            column = column + jnp.where(at_end, ending, 0.0)
            mine = lane == 2 * j + k
            col_s[at, :] = jnp.where(mine, column, col_s[at, :])
            direct_s[at, :] = jnp.where(mine, side(touching), direct_s[at, :])
            skip_s[...] += jnp.where(mine[:8, :], side_row(skipped), 0.0)
        if c > 0:
            later = keep[span - 1 : span, :] * later + mm(c_vals, kept_low, TN)

    @pl.when(j == pl.num_programs(0) - 1)
    def end():
        upper = triangle(span, False)
        rate = jnp.exp(alog_ref[...])
        bias_sum = jnp.zeros((1, MH), F32)
        log_sum = jnp.zeros((1, MH), F32)
        for c in range(count):
            at = slice(c * span, (c + 1) * span)
            mask = same_lower(segc_ref[at, :], segr_ref[:, at], span, True)
            d_inner = jnp.where(mask, d_inner_s[c], 0.0).astype(BF16)
            db_ref[at, :] = (db_s[at, :] + mm(d_inner, c_ref[at, :])).astype(BF16)
            dc_ref[at, :] = (dc_s[at, :] + mm(d_inner, b_ref[at, :], TN)).astype(BF16)
            d_cum = col_s[at, :] + jnp.transpose(row_s[:, at])
            d_log = mm(upper, d_cum, precision=HIGH)[:, :MH]
            dt = pack_ref[at, :MH]
            d_dt = direct_s[at, :MH] - rate * d_log
            d_raw = d_dt * jax.nn.sigmoid(dtr_ref[at, :] + bias_ref[...])
            ddt_ref[at, :] = d_raw.astype(BF16)
            bias_sum = bias_sum + jnp.sum(d_raw, axis=0, keepdims=True)
            log_sum = log_sum - jnp.sum(d_log * dt, axis=0, keepdims=True) * rate
        sums_ref[0:1, :] = bias_sum
        sums_ref[1:2, :] = log_sum
        sums_ref[2:3, :] = skip_s[0:1, :MH]


def ssm_back(
    pack, flip, seg_col, seg_row, x, dy, b_vals, c_vals, skip_wide, enter, leave, dt_raw, bias,
    a_log, after=(),
):
    rows = x.shape[0]
    span = chunk_of(rows)
    square = pltpu.VMEM((rows // span, span, span), F32)
    tall = pltpu.VMEM((rows, LANES), F32)
    return pl.pallas_call(
        behind(ssm_back_kernel, 14, len(after)),
        grid=(PAIRS,),
        out_shape=(
            jax.ShapeDtypeStruct((rows, D_SSM), BF16),
            jax.ShapeDtypeStruct((rows, ST), BF16),
            jax.ShapeDtypeStruct((rows, ST), BF16),
            jax.ShapeDtypeStruct((rows, MH), BF16),
            jax.ShapeDtypeStruct((3, MH), F32),
        ),
        in_specs=[
            held(pack.shape),
            held(flip.shape),
            held(seg_col.shape),
            held(seg_row.shape),
            pair_block(rows),
            pair_block(rows),
            held(b_vals.shape),
            held(c_vals.shape),
            pair_block(1),
            pair_block(ST),
            pair_block(ST),
            held(dt_raw.shape),
            held(bias.shape),
            held(a_log.shape),
        ]
        + anywhere(len(after)),
        out_specs=(
            pair_block(rows),
            held((rows, ST)),
            held((rows, ST)),
            held((rows, MH)),
            held((3, MH)),
        ),
        scratch_shapes=[
            square, square, tall, pltpu.VMEM((LANES, rows), F32), tall, tall, tall,
            pltpu.VMEM((8, LANES), F32),
        ],
        compiler_params=params("arbitrary"),
        name="ssm_back",
    )(
        pack, flip, seg_col, seg_row, x, dy, b_vals, c_vals, skip_wide, enter, leave, dt_raw,
        bias, a_log, *after,
    )


def gather_rows(shard):
    groups = lax.axis_size("ctx")
    part = shard.shape[0] // groups
    own = lax.dynamic_slice_in_dim(shard, lax.axis_index("ctx") * part, part, 0)
    return lax.all_gather(own, ("fsdp", "ctx"), axis=0, tiled=True)


def from_before(value, distance):
    count = lax.axis_size("ctx")
    return lax.ppermute(value, "ctx", [(i, i + distance) for i in range(count - distance)])


def from_after(value, distance):
    count = lax.axis_size("ctx")
    return lax.ppermute(value, "ctx", [(i + distance, i) for i in range(count - distance)])


def across(value, axis, bit):
    count = lax.axis_size(axis)
    return lax.ppermute(value, axis, [(i, i ^ bit) for i in range(count)])


def pick(value, index, axis):
    return lax.dynamic_index_in_dim(value, index, axis, keepdims=False)


def sum_everywhere(value):
    for axis in ("fsdp", "ctx"):
        bit = 1
        while bit < lax.axis_size(axis):
            value = value + across(value, axis, bit)
            bit *= 2
    return value


def reduce_rows(grad):
    share = lax.psum_scatter(grad, "fsdp", scatter_dimension=0, tiled=True)
    return lax.psum(share, "ctx").astype(F32)


def spread_kernel(where_ref, *refs, shapes):
    many = len(shapes)
    owns, theirs, outs = refs[:many], refs[many : 2 * many], refs[2 * many :]
    send_top, keep_top, send_low, keep_low = outs
    y, x = where_ref[1], where_ref[2]
    base = 0
    for own, their, (part, columns) in zip(owns, theirs, shapes):
        for col in range(0, columns, LANES):
            at = slice(col, min(col + LANES, columns))
            wide = at.stop - at.start
            to = slice(base, base + part)

            def total(h, iy, ix):
                left = own[h, 0, iy, ix, :, at].astype(F32)
                return (left + their[h, 0, iy, ix, :, at].astype(F32)).astype(BF16)

            for e in range(2):
                send_top[0, e, to, :wide] = total(0, 1 - y, e)
                keep_top[0, e, to, :wide] = total(0, y, e)
                send_low[0, e, to, :wide] = total(1, e, 1 - x)
                keep_low[0, e, to, :wide] = total(1, e, x)
            base += part


def lanes_of(columns):
    return -(-columns // LANES)


def spread(where, owns, theirs):
    shapes = [a.shape[-2:] for a in owns]
    height = sum(part * lanes_of(columns) for part, columns in shapes)
    halves = owns[0].shape[0] // 2
    split = [a.reshape((2, halves) + a.shape[1:]) for a in (*owns, *theirs)]
    out = jax.ShapeDtypeStruct((halves, 2, height, LANES), BF16)
    out_block = pl.BlockSpec((1, 2, height, LANES), lambda i: (i, 0, 0, 0))
    return pl.pallas_call(
        functools.partial(spread_kernel, shapes=shapes),
        grid=(halves,),
        out_shape=(out,) * 4,
        in_specs=[smem()]
        + [
            pl.BlockSpec((2, 1) + a.shape[2:], lambda i: (0, i, 0, 0, 0, 0))
            for a in split
        ],
        out_specs=(out_block,) * 4,
        compiler_params=params("arbitrary"),
        name="spread",
    )(where, *split)


def narrow_kernel(where_ref, kt, rt, kl, rl, send_top, keep_top, send_low, keep_low):
    y, x = where_ref[1], where_ref[2]
    for keep, got, at, send_out, keep_out in (
        (kt, rt, x, send_top, keep_top),
        (kl, rl, y, send_low, keep_low),
    ):
        for target, index in ((send_out, 1 - at), (keep_out, at)):
            total = keep[0, index].astype(F32) + got[0, index].astype(F32)
            target[0] = total.astype(BF16)


def narrow(where, keep_top, got_top, keep_low, got_low):
    halves, _, height, _ = keep_top.shape
    out = jax.ShapeDtypeStruct((halves, height, LANES), BF16)
    in_block = pl.BlockSpec((1, 2, height, LANES), lambda i: (i, 0, 0, 0))
    out_block = pl.BlockSpec((1, height, LANES), lambda i: (i, 0, 0))
    return pl.pallas_call(
        narrow_kernel,
        grid=(halves,),
        out_shape=(out,) * 4,
        in_specs=[smem()] + [in_block] * 4,
        out_specs=(out_block,) * 4,
        compiler_params=params("arbitrary"),
        name="narrow",
    )(where, keep_top, got_top, keep_low, got_low)


def line_kernel(where_ref, kt, rt, kl, rl, *outs):
    z = where_ref[0]
    halves = kt.shape[0]
    count = 2 * halves
    for i in range(halves):
        for half, (keep, got) in enumerate(((kt, rt), (kl, rl))):
            total = (keep[i].astype(F32) + got[i].astype(F32)).astype(BF16)
            for d in range(count):

                @pl.when(lax.rem(z + d, count) == half * halves + i)
                def store():
                    outs[d][...] = total


def line(where, keep_top, got_top, keep_low, got_low):
    halves, height, _ = keep_top.shape
    out = jax.ShapeDtypeStruct((height, LANES), BF16)
    return pl.pallas_call(
        line_kernel,
        out_shape=(out,) * (2 * halves),
        in_specs=[smem()] + [whole()] * 4,
        out_specs=(whole(),) * (2 * halves),
        compiler_params=params(),
        name="line",
    )(where, keep_top, got_top, keep_low, got_low)


def total_kernel(*refs):
    total = refs[0][...].astype(F32)
    for ref in refs[1:-1]:
        total = total + ref[...].astype(F32)
    refs[-1][...] = total.astype(BF16)


def total_of(pieces):
    return pl.pallas_call(
        total_kernel,
        out_shape=jax.ShapeDtypeStruct(pieces[0].shape, BF16),
        in_specs=[whole()] * len(pieces),
        out_specs=whole(),
        compiler_params=params(),
        name="total",
    )(*pieces)


def place_kernel(where_ref, *refs, shapes, count):
    parts, outs = refs[:count], refs[count:]
    place = 2 * where_ref[1] + where_ref[2]
    for d, ref in enumerate(parts):
        base = 0
        for out, (part, columns) in zip(outs, shapes):
            rows = pl.ds(pl.multiple_of((place ^ d) * part, part), part)
            for col in range(0, columns, LANES):
                at = slice(col, min(col + LANES, columns))
                out[rows, at] = ref[base : base + part, : at.stop - at.start].astype(F32)
                base += part


def place_rows(where, pieces, shapes):
    count = len(pieces)
    return pl.pallas_call(
        functools.partial(place_kernel, shapes=shapes, count=count),
        out_shape=tuple(jax.ShapeDtypeStruct((count * r, c), F32) for r, c in shapes),
        in_specs=[smem()] + [whole()] * count,
        out_specs=(whole(),) * len(shapes),
        compiler_params=params(),
        name="place_rows",
    )(where, *pieces)


def along_z(value, distance):
    count = lax.axis_size("fsdp")
    hop = 2 * distance
    return lax.ppermute(value, "fsdp", [(i, (i + hop) % count) for i in range(count)])


class Reduction:
    def __init__(self, where, owns, theirs):
        self.where = where
        self.owns = owns
        self.shapes = [a.shape[-2:] for a in owns]
        self.theirs = [across(a, "fsdp", 1) for a in theirs]

    def spread(self):
        send_top, self.keep_top, send_low, self.keep_low = spread(
            self.where, self.owns, self.theirs
        )
        self.got_top, self.got_low = across(send_top, "ctx", 2), across(send_low, "ctx", 1)
        return self.keep_top

    def narrow(self):
        send_top, self.keep_top, send_low, self.keep_low = narrow(
            self.where, self.keep_top, self.got_top, self.keep_low, self.got_low
        )
        self.got_top, self.got_low = across(send_top, "ctx", 1), across(send_low, "ctx", 2)
        return self.keep_top

    def line(self):
        pieces = line(self.where, self.keep_top, self.got_top, self.keep_low, self.got_low)
        self.pieces = [pieces[0]] + [along_z(p, d) for d, p in enumerate(pieces) if d]
        return pieces[0]

    def total(self):
        share = total_of(self.pieces)
        self.shares = [share] + [across(share, "ctx", d) for d in range(1, 4)]
        return share

    def finish(self):
        return place_rows(self.where, self.shares, self.shapes)


def rms_forward(value_rows, gain):
    inverse = lax.rsqrt(jnp.mean(value_rows * value_rows, axis=-1, keepdims=True) + EPS)
    return (value_rows * inverse * gain, inverse)


def rms_backward(value_rows, inverse, gain, grad):
    weighted = grad * gain
    gain_grad = jnp.sum(grad * value_rows * inverse, axis=0)
    inner = jnp.mean(weighted * value_rows, axis=-1, keepdims=True)
    return (inverse * weighted - value_rows * inverse * inverse * inverse * inner, gain_grad)


def rope_tables(positions):
    half = HEAD_WIDTH // 2
    lane = jnp.arange(LANES)
    freqs = ROPE_BASE ** (-((lane % half).astype(F32) * 2.0) / HEAD_WIDTH)
    angles = positions.astype(F32)[:, None] * freqs[None, :]
    sign = jnp.where(lane % HEAD_WIDTH < half, -1.0, 1.0)
    return (jnp.cos(angles), jnp.sin(angles) * sign[None, :])


def chain(packed):
    state = jnp.zeros((ST, D_SSM), F32)
    for item in reversed(packed):
        own = item.astype(F32)
        flow = own[ST : ST + 1] + own[ST + 1 : ST + 2] + own[ST + 2 : ST + 3]
        state = own[:ST] + flow * state
    return state


def dotf(left, right):
    return jnp.dot(left, right, preferred_element_type=F32)


def shards(
    hidden_in, seg_ids, gain_mixer, gain_ffn, w_in, w_qkv, w_attn_out, w_ssm_out, w_gate_up,
    w_down, dt_bias, a_log, d_skip, out_grad,
):
    rows = hidden_in.shape[0]
    groups = lax.axis_size("ctx")
    place = lax.axis_index("ctx")
    full_first = gather_rows(jnp.concatenate([w_qkv, w_in], axis=1))
    full_attn_out = gather_rows(w_attn_out)
    full_ssm_out = gather_rows(w_ssm_out)
    full_gate_up = gather_rows(w_gate_up)
    full_down = gather_rows(w_down)

    seg_before = [seg_ids] + [from_before(seg_ids, k) for k in range(1, groups)]
    start = jnp.zeros((rows,), jnp.int32)
    for k in range(groups):
        earlier = (seg_before[k][None, :] < seg_ids[:, None]) & (k <= place)
        start = start + jnp.sum(earlier.astype(jnp.int32), axis=1)
    positions = place * rows + jnp.arange(rows, dtype=jnp.int32) - start
    prev_seg = jnp.where(place > 0, seg_before[1][-1:], -1).astype(jnp.int32)
    place_array = place.astype(jnp.int32).reshape(1)
    start_row = start.reshape(1, rows)
    seg_col = seg_ids.reshape(rows, 1)
    seg_row = seg_ids.reshape(1, rows)
    bias = dt_bias.reshape(1, MH)
    rates = a_log.reshape(1, MH)
    skip_wide = jnp.repeat(d_skip, PD).reshape(1, D_SSM)
    cos, sin = rope_tables(positions)

    inputs = hidden_in.astype(F32)
    normed, inverse_mixer = rms_forward(inputs, gain_mixer)
    normed_low = normed.astype(BF16)
    qkv_cols = w_qkv.shape[1]
    at_z, at_xbc = qkv_cols, qkv_cols + D_SSM
    at_dt = at_xbc + D_SSM + 2 * ST
    qkv = dotf(normed_low, full_first[:, :at_z])
    xbc = dotf(normed_low, full_first[:, at_xbc:at_dt]).astype(BF16)
    ssm_x, ssm_b, ssm_c = xbc[:, :D_SSM], xbc[:, D_SSM : D_SSM + ST], xbc[:, D_SSM + ST :]
    dt_raw = dotf(normed_low, full_first[:, at_dt:])
    gate_z = dotf(normed_low, full_first[:, at_z:at_xbc])
    q, kv = rotate(qkv, cos, sin)
    kv_all = jnp.stack([kv] + [from_before(kv, k) for k in range(1, groups)])
    pack, flip, far, end_state = ssm_state(prev_seg, dt_raw, bias, rates, seg_col, ssm_x, ssm_b)
    enter = chain([from_before(end_state, k) for k in range(1, groups)])

    attended, lse = attend(place_array, q, kv_all, start_row)
    attended_low = attended.astype(BF16)
    gated_low, y = ssm_forward(
        pack, flip, seg_col, seg_row, ssm_x, ssm_b, ssm_c, gate_z, skip_wide, enter
    )
    middle = inputs + dotf(attended_low, full_attn_out) + dotf(gated_low, full_ssm_out)
    normed_ffn, inverse_ffn = rms_forward(middle, gain_ffn)
    normed_ffn_low = normed_ffn.astype(BF16)
    gate = dotf(normed_ffn_low, full_gate_up[:, :FF])
    up = dotf(normed_ffn_low, full_gate_up[:, FF:])
    sigmoid_gate = jax.nn.sigmoid(gate)
    hidden_low = (gate * sigmoid_gate * up).astype(BF16)
    output = (middle + dotf(hidden_low, full_down)).astype(BF16)

    staged = groups == 4 and lax.axis_size("fsdp") == 8
    fsdp_place = lax.axis_index("fsdp")
    core = fsdp_place % 2
    where = jnp.stack([fsdp_place // 2, place // 2, place % 2]).astype(jnp.int32)

    def sides(left):
        width = left.shape[1] // lax.axis_size("fsdp")
        split = left.reshape(rows, -1, 2, width)
        return tuple(pick(split, k, 2).reshape(rows, -1) for k in (core, 1 - core))

    def split(grad):
        lines, part = lax.axis_size("fsdp") // 2, grad.shape[0] // 16
        return grad.reshape(lines, 2, 2, part, grad.shape[1])

    def product(own_other, right):
        own, other = own_other
        theirs = split(dotf(other.T, right).astype(BF16))
        return (split(dotf(own.T, right).astype(BF16)), theirs)

    def parted(left, right):
        grad = dotf(left.T, right).astype(BF16)
        both = grad.reshape(-1, 2, 2, 2, grad.shape[0] // 32, grad.shape[1])
        return (pick(both, core, 1), pick(both, 1 - core, 1))

    def begin(pairs):
        owns, theirs = zip(*pairs, strict=True)
        return Reduction(where, owns, theirs)

    hold = lambda step: (step(),) if staged else ()
    normed_sides = sides(normed_low)
    d_hidden = dotf(out_grad, full_down.T)
    d_gate = (d_hidden * up * sigmoid_gate * (1.0 + gate * (1.0 - sigmoid_gate))).astype(BF16)
    d_up = (d_hidden * gate * sigmoid_gate).astype(BF16)
    d_gate_up = jnp.concatenate([d_gate, d_up], axis=1)
    if staged:
        one = begin(
            [product(sides(hidden_low), out_grad), product(sides(normed_ffn_low), d_gate_up)]
        )
    d_normed_ffn = dotf(d_gate_up, full_gate_up.T)
    middle_part, grad_gain_ffn = rms_backward(middle, inverse_ffn, gain_ffn, d_normed_ffn)
    d_middle = out_grad.astype(F32) + middle_part
    d_branch = d_middle.astype(BF16)
    d_attended = dotf(d_branch, full_attn_out.T).astype(BF16)
    d_gated = dotf(d_branch, full_ssm_out.T).astype(BF16)

    dz, dy, state_grad = ssm_gate_back(far, d_gated, y, gate_z, ssm_c, end_state[ST:])
    leave = chain([from_after(state_grad, k) for k in range(1, groups)])
    if staged:
        two = begin(
            [
                parted(attended_low, d_branch),
                parted(gated_low, d_branch),
                product(normed_sides, dz),
            ]
        )
    dq, dkv_all = attend_back(
        place_array, q, kv_all, start_row, lse, attended, d_attended,
        after=hold(lambda: one.spread()),
    )
    dkv = dkv_all[0].astype(F32)
    for k in range(1, groups):
        dkv = dkv + from_after(dkv_all[k], k).astype(F32)
    dx, db, dc, ddt, sums = ssm_back(
        pack, flip, seg_col, seg_row, ssm_x, dy, ssm_b, ssm_c, skip_wide, enter, leave, dt_raw,
        bias, rates, after=hold(lambda: one.narrow()) + hold(lambda: two.spread()),
    )
    d_qkv = unrotate(dq, dkv, cos, sin)
    d_late = jnp.concatenate([dx, db, dc, ddt], axis=1)
    if staged:
        three = begin([product(normed_sides, d_qkv), product(normed_sides, d_late)])
        one.line()
        two.narrow()
        three.spread()
    d_early = jnp.concatenate([d_qkv, dz], axis=1)
    d_normed = dotf(d_early, full_first[:, :at_xbc].T) + dotf(d_late, full_first[:, at_xbc:].T)
    input_part, grad_gain_mixer = rms_backward(inputs, inverse_mixer, gain_mixer, d_normed)
    grad_input = d_middle + input_part
    small = jnp.concatenate([sums.reshape(-1), grad_gain_mixer, grad_gain_ffn])
    small = sum_everywhere(small)
    head_sums = small[: 3 * MH].reshape(3, MH)
    gains = small[3 * MH :].reshape(2, lax.axis_size("fsdp"), -1)
    gains = pick(gains, fsdp_place, 1)
    if staged:
        one.total()
        two.line()
        three.narrow()
        two.total()
        three.line()
        three.total()
        out_down, out_gate_up = one.finish()
        out_attn, out_ssm, out_z = two.finish()
        out_qkv, out_late = three.finish()
    else:
        out_down = reduce_rows(dotf(hidden_low.T, out_grad).astype(BF16))
        out_gate_up = reduce_rows(dotf(normed_ffn_low.T, d_gate_up).astype(BF16))
        out_attn = reduce_rows(dotf(attended_low.T, d_branch).astype(BF16))
        out_ssm = reduce_rows(dotf(gated_low.T, d_branch).astype(BF16))
        out_z = reduce_rows(dotf(normed_low.T, dz).astype(BF16))
        out_qkv = reduce_rows(dotf(normed_low.T, d_qkv).astype(BF16))
        out_late = reduce_rows(dotf(normed_low.T, d_late).astype(BF16))
    return (
        output,
        grad_input,
        gains[0],
        gains[1],
        jnp.concatenate([out_z, out_late], axis=1),
        out_qkv,
        out_attn,
        out_ssm,
        out_gate_up,
        out_down,
        head_sums[0],
        head_sums[1],
        head_sums[2],
    )


def solution(mesh):
    tokens = P(("fsdp", "ctx"), None)
    weight = P("fsdp", None)
    return jax.shard_map(
        shards,
        mesh=mesh,
        in_specs=(
            tokens, P(("fsdp", "ctx")), P(), P(), weight, weight, weight, weight, weight, weight,
            P(), P(), P(), tokens,
        ),
        out_specs=(
            tokens, tokens, P("fsdp"), P("fsdp"), weight, weight, weight, weight, weight, weight,
            P(), P(), P(),
        ),
        check_vma=False,
    )
```

time: 1320 us -> 773 us (0.59)
  matrix products: 308 us -> 111 us
  local copies, waits for them, and re-layouts: 279 us -> 92.5 us
  waiting for transfers between devices: 444 us -> 297 us
  Pallas kernels: 0 us -> 138 us
  other arithmetic: 123 us -> 21.4 us
  blocking collectives: 100 us -> 0 us
  starting transfers between devices: 0.89 us -> 84.6 us
  loops' own time: 30.8 us -> 0 us
    reduce_scatter x7 -> x0, waiting for transfers between devices: 248 us -> none  [the longest x1 89.9 us: shards(): lax.psum_scatter(gradients[4].astype(jnp.bfloat16), 'fsdp', scatter_dimen...]
    dot_general x59 -> x27, matrix products: 308 us -> 111 us  [dotf(): return jnp.dot(left, right, preferred_element_type=F32)]
    dynamic_update_slice x22 -> x0, local copies, waits for them, and re-layouts: 148 us -> none  [ssd_blocks(): (state, last), results = lax.scan(step, init, items)]
    pallas_call x0 -> x23, Pallas kernels: none -> 138 us  [the longest x1 29.3 us: ssm_back(): pl.pallas_call(behind(ssm_back_kernel, 14, len(after)), grid=(PAIRS,), ou...]
    ppermute x0 -> x57, starting transfers between devices: none -> 84.4 us  [the longest x33 34.2 us: across(): return lax.ppermute(value, axis, [(i, i ^ bit) for i in range(count)])]
    ppermute x0 -> x57, waiting for transfers between devices: none -> 81.1 us  [the longest x33 31.3 us: across(): return lax.ppermute(value, axis, [(i, i ^ bit) for i in range(count)])]
    all_gather x8 -> x5, waiting for transfers between devices: 141 us -> 216 us  [gather_rows(): return lax.all_gather(own, ('fsdp', 'ctx'), axis=0, tiled=True)]
    psum x2 -> x0, blocking collectives: 47.5 us -> none  [the longest x1 38.4 us: shards(): lax.psum((dt_bias_grad, a_log_grad, d_skip_grad), ('fsdp', 'ctx'))]
  transfers between devices with their start and end apart: 17 -> 62, of which waited for: 10 -> 18; matrix products, arithmetic and copies ran while one was open for 49% -> 22% of each run, Pallas kernels for 0% -> 18%
where the time goes in v1:
time: 773 us; the launch traced here: 761 us
  waiting for transfers between devices  297 us (38%)
  Pallas kernels  138 us (18%)
  matrix products  111 us (14%)
  local copies, waits for them, and re-layouts  92.5 us (12%)
  starting transfers between devices  84.6 us (11%)
  other arithmetic  21.4 us (3%)
  between operations  15.6 us (2%)
    all_gather x5, waiting for transfers between devices, gather_rows(): return lax.all_gather(own, ('fsdp', 'ctx'), axis=0, tiled=True)  216 us
    dot_general x27, matrix products, dotf(): return jnp.dot(left, right, preferred_element_type=F32)  111 us
    unnamed x139, local copies, waits for them, and re-layouts  42.8 us
    ppermute x33, starting transfers between devices, across(): return lax.ppermute(value, axis, [(i, i ^ bit) for i in range(count)])  34.2 us
    ppermute x33, waiting for transfers between devices, across(): return lax.ppermute(value, axis, [(i, i ^ bit) for i in range(count)])  31.3 us
    pallas_call x1, Pallas kernels, ssm_back(): pl.pallas_call(behind(ssm_back_kernel, 14, len(after)), grid=(PAIRS,), ou...  29.3 us
    ppermute x9, waiting for transfers between devices, from_before(): lax.ppermute(value, 'ctx', [(i, i + distance) for i in range(count - dist...  24.7 us
    ppermute x9, starting transfers between devices, from_before(): lax.ppermute(value, 'ctx', [(i, i + distance) for i in range(count - dist...  21.5 us
  transfers between devices with their start and end apart: 62, of which 18 were waited for; matrix products, arithmetic and copies ran while one was open for 22% of the time, Pallas kernels for 18%

profile of v1, /device:TPU:0, one launch (start us, length us, event | category | flops | bytes accessed | tf_op | source)
XLA Modules:
  0.0 761.3 jit_solution(9165377799997937789)
XLA Ops:
  15.4 4.8 collective-permute-start
  20.2 3.4 collective-permute-start.1
  26.4 3.5 constant_dynamic-slice_fusion.2
  31.5 3.5 copy.99
  39.4 36.8 %all-gather.14.cloned.1.call-done = bf16[2048,1024]{1,0:T(8,128)(2,1)} async-done(((bf16[64,1024]{1,0:T(8,128)(2,1)}), bf16[2048,1024]{1,0:T(8,128)(2,1)}) %all-gather.14.cloned.1.call-update) | async-done | bytes 4194320 | tf_op jit(solution)/shard_map/all_gather | solution.py:691
  76.3 6.6 fusion.82
  82.8 74.0 %all-gather.6.cloned.1.call-done = bf16[1024,4120]{1,0:T(8,128)(2,1)} async-done(((bf16[32,4120]{1,0:T(8,128)(2,1)}), bf16[1024,4120]{1,0:T(8,128)(2,1)}) %all-gather.6.cloned.1.call-update) | async-done | bytes 8437776 | tf_op jit(solution)/shard_map/all_gather | solution.py:691
  156.8 4.1 fusion.17
  162.2 3.5 fusion.35.qkv_ref
  165.7 3.1 rotate.1
  168.8 3.7 collective-permute-start.5
  175.3 5.4 ssm_state.1
  190.4 5.5 fusion.15.z_ref
  195.9 24.7 %collective-permute-done.4 = bf16[2,512,128]{2,1,0:T(8,128)(2,1)S(1)} collective-permute-done((bf16[2,512,128]{2,1,0:T(8,128)(2,1)S(1)}, bf16[2,512,128]{2,1,0:T(8,128)(2,1)S(1)}, u32[]{:S(2)}, u32[]{:S(2)}) %collective-permute-start.4) | collective-permute-done | bytes 262176 | tf_op jit(solution)/shard_map/ppermute | solution.py:696
  221.7 7.5 attend.1
  230.7 14.7 %ssm_forward.1 = (bf16[512,1536]{1,0:T(8,128)(2,1)}, f32[512,1536]{1,0:T(8,128)}) custom-call(f32[512,128]{1,0:T(8,128)} %get-tuple-element.79.pack_ref.refs_0_, f32[128,512]{1,0:T(8,128)} %get-tuple-element.80.flip_ref.refs_1_, s32[512,1]{1,0:T(8,128)} %copy.74.seg_ref.segc_ref.refs_2_, s32[1,512]{1,0:T(1,128)} %bitcast.141, ...), custom_call_target="tpu_custom_call" | custom-call | tf_op jit(solution)/shard_map/ssm_forward/pallas_call | solution.py:441
  245.4 5.5 fusion.81
  250.9 32.5 %all-gather.8.cloned.1.call-done = bf16[512,1024]{1,0:T(8,128)(2,1)} async-done(((bf16[16,1024]{1,0:T(8,128)(2,1)}), bf16[512,1024]{1,0:T(8,128)(2,1)}) %all-gather.8.cloned.1.call-update) | async-done | bytes 1048592 | tf_op jit(solution)/shard_map/all_gather | solution.py:691
  283.3 3.1 multiply_reduce_fusion.2
  290.2 72.8 %all-gather.12.cloned.1.call-done = bf16[1024,4096]{1,0:T(8,128)(2,1)} async-done(((bf16[32,4096]{1,0:T(8,128)(2,1)}), bf16[1024,4096]{1,0:T(8,128)(2,1)}) %all-gather.12.cloned.1.call-update) | async-done | bytes 8388624 | tf_op jit(solution)/shard_map/all_gather | solution.py:691
  363.1 5.0 fusion.4
  369.5 5.6 fusion.8
  375.1 4.9 reshape.249
  380.0 8.6 %constant_dynamic-slice_fusion.7 = (bf16[512,4,1,256]{3,2,1,0:T(2,128)(2,1)}, bf16[512,4,1,256]{3,2,1,0:T(2,128)(2,1)}) fusion(bf16[512,4,2,256]{3,2,1,0:T(2,128)(2,1)} %reshape.249, s32[]{:T(128)S(6)} %select_n.101, s32[]{:T(128)S(6)} %select_n.100), kind=kLoop, calls=%fused_computation.133 | loop fusion | bytes 4194312 | tf_op jit(solution)/shard_map/jit(dynamic_index_in_dim)/dynamic_slice | solution.py:710
  388.6 3.5 constant_dynamic-slice_fusion.6
  392.2 5.8 copy.94
  398.0 4.1 convolution_convert_fusion.8
  402.3 3.6 copy.95
  406.0 6.9 convolution_convert_fusion
  413.2 8.3 %multiply_reduce_fusion = (f32[1024]{0:T(1024)S(1)}, f32[512]{0:T(512)S(1)}, f32[512,1024]{1,0:T(8,128)S(1)}) fusion(f32[512,1024]{1,0:T(8,128)S(1)} %get-tuple-element.227, f32[512]{0:T(512)S(1)} %add_rsqrt_fusion, f32[1024]{0:T(1024)S(1)} %copy-done.48, bf16[1024,4096]{1,0:T(8,128)(2,1)} %all-gather.12.cloned.1.call-done, ...), kind=kOutput, calls=%fused_computation.51 | convolution fusion | flops 4306500096 | bytes 16789504 | tf_op jit(solution)/shard_map/dot_general | solution.py:946
  431.5 11.3 %ssm_gate_back.1 = (bf16[512,1536]{1,0:T(8,128)(2,1)}, bf16[512,1536]{1,0:T(8,128)(2,1)}, bf16[144,1536]{1,0:T(8,128)(2,1)}) custom-call(f32[512,128]{1,0:T(8,128)} %get-tuple-element.87.far_ref, bf16[512,1536]{1,0:T(8,128)(2,1)} %convolution_convert_fusion.7.dg_ref, f32[512,1536]{1,0:T(8,128)} %get-tuple-element.88.y_ref, f32[512,1536]{1,0:T(8,128)} %fusion.15.z_ref, ...), custom_call_target="tpu_custom_call" | custom-call | tf_op jit(solution)/shard_map/ssm_gate_back/pallas_call | solution.py:485
  442.8 3.6 convolution_convert_fusion.3
  448.9 3.5 copy.98
  453.0 3.5 copy.93
  456.4 3.8 convolution_convert_fusion.4
  462.9 4.9 spread.4
  467.7 3.4 collective-permute-start.27
  473.4 4.4 convolution_convert_fusion.1
  477.8 5.8 copy.92
  484.9 4.1 convolution_convert_fusion.9
  489.0 8.3 %spread.3 = (bf16[2,2,1536,128]{3,2,1,0:T(8,128)(2,1)}, bf16[2,2,1536,128]{3,2,1,0:T(8,128)(2,1)}, bf16[2,2,1536,128]{3,2,1,0:T(8,128)(2,1)}, bf16[2,2,1536,128]{3,2,1,0:T(8,128)(2,1)}) custom-call(s32[3]{0:T(128)} %pad_add_fusion.where_ref, bf16[2,2,2,2,64,1024]{5,4,3,2,1,0:T(8,128)(2,1)} %bitcast.122, bf16[2,2,2,2,32,4096]{5,4,3,2,1,0:T(8,128)(2,1)} %bitcast.120, ...), custom_call_target="tpu_custom_call" | custom-call | tf_op jit(solution)/shard_map/spread/pallas_call | solution.py:762
  504.9 3.1 narrow.4
  508.0 3.2 collective-permute-start.29
  511.2 12.9 %attend_back.1 = (f32[512,512]{1,0:T(8,128)}, bf16[4,2,512,128]{3,2,1,0:T(8,128)(2,1)}) custom-call(s32[1]{0:T(128)} %bitcast.place_ref.refs_0_, bf16[512,512]{1,0:T(8,128)(2,1)} %get-tuple-element.76.q_ref.refs_1_, bf16[4,2,512,128]{3,2,1,0:T(8,128)(2,1)} %pad_maximum_fusion.5.kv_ref.refs_2_, s32[1,512]{1,0:T(1,128)} %bitcast.145, ...), custom_call_target="tpu_custom_call" | custom-call | tf_op jit(solution)/shard_map/attend_back/pallas_call | solution.py:261
  527.5 19.3 %collective-permute-done.29.rt = bf16[2,896,128]{2,1,0:T(8,128)(2,1)S(1)} collective-permute-done((bf16[2,896,128]{2,1,0:T(8,128)(2,1)}, bf16[2,896,128]{2,1,0:T(8,128)(2,1)S(1)}, u32[]{:S(2)}, u32[]{:S(2)}) %collective-permute-start.29) | collective-permute-done | bytes 458784 | tf_op jit(solution)/shard_map/ppermute | solution.py:706
  555.6 4.0 collective-permute-done.12
  563.5 3.2 unrotate.1
  567.9 4.4 narrow.3
  572.4 29.3 %ssm_back.1 = (bf16[512,1536]{1,0:T(8,128)(2,1)}, bf16[512,128]{1,0:T(8,128)(2,1)}, bf16[512,128]{1,0:T(8,128)(2,1)}, bf16[512,24]{1,0:T(8,128)(2,1)}, f32[3,24]{1,0:T(4,128)}) custom-call(f32[512,128]{1,0:T(8,128)} %get-tuple-element.79.pack_ref.refs_0_, f32[128,512]{1,0:T(8,128)} %get-tuple-element.80.flip_ref.refs_1_, ...), custom_call_target="tpu_custom_call" | custom-call | tf_op jit(solution)/shard_map/ssm_back/pallas_call | solution.py:641
  607.1 3.9 copy.88
  615.9 5.2 fusion.11
  621.2 6.6 fusion.34
  630.6 4.2 convolution_convert_fusion.6
  634.7 4.1 copy.87
  638.8 3.9 spread.5
  645.5 3.1 collective-permute-done.23
  650.6 4.3 collective-permute-done.33.refs_3_
  666.1 3.8 line.5
  678.7 5.5 add_convert_fusion
  689.1 9.6 %collective-permute-done.52.refs_2_ = bf16[1536,128]{1,0:T(8,128)(2,1)S(1)} collective-permute-done((bf16[1536,128]{1,0:T(8,128)(2,1)}, bf16[1536,128]{1,0:T(8,128)(2,1)S(1)}, u32[]{:S(2)}, u32[]{:S(2)}) %collective-permute-start.52) | collective-permute-done | bytes 393248 | tf_op jit(solution)/shard_map/ppermute | solution.py:877
  706.6 8.8 %collective-permute-start.43 = (bf16[672,128]{1,0:T(8,128)(2,1)}, bf16[672,128]{1,0:T(8,128)(2,1)S(1)}, u32[]{:S(2)}, u32[]{:S(2)}) collective-permute-start(bf16[672,128]{1,0:T(8,128)(2,1)} %get-tuple-element.123), channel_id=1, source_target_pairs={{0,8},{4,12},{8,16},{12,20},{16,24},{20,28},{24,0},{28,4},{1,9},{5... | collective-permute-start | bytes 516104 | tf_op jit(solution)/shard_map/ppermute | solution.py:877
  715.3 3.8 fusion.29
  724.4 6.7 collective-permute-done.44.refs_2_
  741.0 3.2 place_rows.5
  (319 shorter events, 157.8 us)
Async XLA Ops:
  7.2 69.1 %all-gather.14.cloned.1.call-start = ((), (), s32[]{:S(2)}) async-start(), calls=%async_computation.4 | async-start | bytes 4325376 | tf_op jit(solution)/shard_map/all_gather | solution.py:691
  9.0 147.9 %all-gather.6.cloned.1.call-start = ((), (), s32[]{:S(2)}) async-start(), calls=%async_computation | async-start | bytes 8921088 | tf_op jit(solution)/shard_map/all_gather | solution.py:691
  11.5 233.9 %all-gather.10.cloned.1.call-start = ((), (), s32[]{:S(2)}) async-start(), calls=%async_computation.2 | async-start | bytes 3244032 | tf_op jit(solution)/shard_map/all_gather | solution.py:691
  13.1 270.2 %all-gather.8.cloned.1.call-start = ((), (), s32[]{:S(2)}) async-start(), calls=%async_computation.1 | async-start | bytes 1081344 | tf_op jit(solution)/shard_map/all_gather | solution.py:691
  14.6 348.5 %all-gather.12.cloned.1.call-start = ((), (), s32[]{:S(2)}) async-start(), calls=%async_computation.3 | async-start | bytes 8650752 | tf_op jit(solution)/shard_map/all_gather | solution.py:691
  15.4 19.7 %collective-permute-start = (s32[512]{0:T(512)S(1)}, s32[512]{0:T(512)S(1)}, u32[]{:S(2)}, u32[]{:S(2)}) collective-permute-start(s32[512]{0:T(512)S(1)} %copy-done.47), channel_id=1, source_target_pairs={{0,1},{1,2},{2,3},{4,5},{5,6},{6,7},{8,9},{9,10},{10,11},{12,13},{... | collective-permute-start | bytes 6152 | tf_op jit(solution)/shard_map/ppermute | solution.py:696
  20.2 16.1 %collective-permute-start.1 = (s32[512]{0:T(512)S(1)}, s32[512]{0:T(512)S(1)}, u32[]{:S(2)}, u32[]{:S(2)}) collective-permute-start(s32[512]{0:T(512)S(1)} %copy-done.47), channel_id=1, source_target_pairs={{0,2},{1,3},{4,6},{5,7},{8,10},{9,11},{12,14},{13,15},{16,18},{17,... | collective-permute-start | bytes 6152 | tf_op jit(solution)/shard_map/ppermute | solution.py:696
  23.7 12.6 %collective-permute-start.2 = (s32[512]{0:T(512)S(1)}, s32[512]{0:T(512)S(1)}, u32[]{:S(2)}, u32[]{:S(2)}) collective-permute-start(s32[512]{0:T(512)S(1)} %copy-done.47), channel_id=1, source_target_pairs={{0,3},{4,7},{8,11},{12,15},{16,19},{20,23},{24,27},{28,31}} | collective-permute-start | bytes 6152 | tf_op jit(solution)/shard_map/ppermute | solution.py:696
  29.9 46.4 %copy-start.7 = (bf16[512,1024]{1,0:T(8,128)(2,1)S(1)}, bf16[512,1024]{1,0:T(8,128)(2,1)}, u32[]{:S(2)}) copy-start(bf16[512,1024]{1,0:T(8,128)(2,1)} %param.27) | copy-start | bytes 3145732
  168.8 19.7 %collective-permute-start.5 = (bf16[2,512,128]{2,1,0:T(8,128)(2,1)}, bf16[2,512,128]{2,1,0:T(8,128)(2,1)S(1)}, u32[]{:S(2)}, u32[]{:S(2)}) collective-permute-start(bf16[2,512,128]{2,1,0:T(8,128)(2,1)} %get-tuple-element.77), channel_id=1, source_target_pairs={{0,3},{4,7},{8,11},{12,15},{16,19},{20,23},{24,27},{28,31}} | collective-permute-start | bytes 786440 | tf_op jit(solution)/shard_map/ppermute | solution.py:696
  180.7 48.5 %collective-permute-start.8 = (bf16[144,1536]{1,0:T(8,128)(2,1)}, bf16[144,1536]{1,0:T(8,128)(2,1)S(1)}, u32[]{:S(2)}, u32[]{:S(2)}) collective-permute-start(bf16[144,1536]{1,0:T(8,128)(2,1)} %get-tuple-element.81), channel_id=1, source_target_pairs={{0,3},{4,7},{8,11},{12,15},{16,19},{20,23},{24,27},{28,31}} | collective-permute-start | bytes 1327112 | tf_op jit(solution)/shard_map/ppermute | solution.py:696
  182.0 47.3 %collective-permute-start.7 = (bf16[144,1536]{1,0:T(8,128)(2,1)}, bf16[144,1536]{1,0:T(8,128)(2,1)S(1)}, u32[]{:S(2)}, u32[]{:S(2)}) collective-permute-start(bf16[144,1536]{1,0:T(8,128)(2,1)} %get-tuple-element.81), channel_id=1, source_target_pairs={{0,2},{1,3},{4,6},{5,7},{8,10},{9,11},{12,14},{13,15},{16,18},{17,... | collective-permute-start | bytes 1327112 | tf_op jit(solution)/shard_map/ppermute | solution.py:696
  183.3 46.1 %collective-permute-start.6 = (bf16[144,1536]{1,0:T(8,128)(2,1)}, bf16[144,1536]{1,0:T(8,128)(2,1)S(1)}, u32[]{:S(2)}, u32[]{:S(2)}) collective-permute-start(bf16[144,1536]{1,0:T(8,128)(2,1)} %get-tuple-element.81), channel_id=1, source_target_pairs={{0,1},{1,2},{2,3},{4,5},{5,6},{6,7},{8,9},{9,10},{10,11},{12,13},{... | collective-permute-start | bytes 1327112 | tf_op jit(solution)/shard_map/ppermute | solution.py:696
  185.8 34.8 %collective-permute-start.4 = (bf16[2,512,128]{2,1,0:T(8,128)(2,1)S(1)}, bf16[2,512,128]{2,1,0:T(8,128)(2,1)S(1)}, u32[]{:S(2)}, u32[]{:S(2)}) collective-permute-start(bf16[2,512,128]{2,1,0:T(8,128)(2,1)S(1)} %copy-done.34), channel_id=1, source_target_pairs={{0,2},{1,3},{4,6},{5,7},{8,10},{9,11},{12,14},{13,15},{16,18},{17,... | collective-permute-start | bytes 786440 | tf_op jit(solution)/shard_map/ppermute | solution.py:696
  188.5 32.1 %collective-permute-start.3 = (bf16[2,512,128]{2,1,0:T(8,128)(2,1)S(1)}, bf16[2,512,128]{2,1,0:T(8,128)(2,1)S(1)}, u32[]{:S(2)}, u32[]{:S(2)}) collective-permute-start(bf16[2,512,128]{2,1,0:T(8,128)(2,1)S(1)} %copy-done.34), channel_id=1, source_target_pairs={{0,1},{1,2},{2,3},{4,5},{5,6},{6,7},{8,9},{9,10},{10,11},{12,13},{... | collective-permute-start | bytes 786440 | tf_op jit(solution)/shard_map/ppermute | solution.py:696
  402.1 69.1 %collective-permute-start.9 = (bf16[4,2,2,64,1024]{4,3,2,1,0:T(8,128)(2,1)}, bf16[4,2,2,64,1024]{4,3,2,1,0:T(8,128)(2,1)}, u32[]{:S(2)}, u32[]{:S(2)}) collective-permute-start(bf16[4,2,2,64,1024]{4,3,2,1,0:T(8,128)(2,1)} %bitcast.20), channel_id=1, source_target_pairs={{0,4},{4,0},{8,12},{12,8},{16,20},{20,16},{24,28},{28,24},{1,5},{5... | collective-permute-start | bytes 6291464 | tf_op jit(solution)/shard_map/ppermute | solution.py:706
  412.9 70.7 %collective-permute-start.10 = (bf16[4,2,2,32,4096]{4,3,2,1,0:T(8,128)(2,1)}, bf16[4,2,2,32,4096]{4,3,2,1,0:T(8,128)(2,1)}, u32[]{:S(2)}, u32[]{:S(2)}) collective-permute-start(bf16[4,2,2,32,4096]{4,3,2,1,0:T(8,128)(2,1)} %bitcast.23), channel_id=1, source_target_pairs={{0,4},{4,0},{8,12},{12,8},{16,20},{20,16},{24,28},{28,24},{1,5},{5... | collective-permute-start | bytes 12582920 | tf_op jit(solution)/shard_map/ppermute | solution.py:706
  427.8 33.7 %collective-permute-start.20 = (bf16[4,2,2,48,1024]{4,3,2,1,0:T(8,128)(2,1)}, bf16[4,2,2,48,1024]{4,3,2,1,0:T(8,128)(2,1)}, u32[]{:S(2)}, u32[]{:S(2)}) collective-permute-start(bf16[4,2,2,48,1024]{4,3,2,1,0:T(8,128)(2,1)} %get-tuple-element.204), channel_id=1, source_target_pairs={{0,4},{4,0},{8,12},{12,8},{16,20},{20,16},{24,28},{28,24},{1,5},{5... | collective-permute-start | bytes 4718600 | tf_op jit(solution)/shard_map/ppermute | solution.py:706
  446.5 16.3 %collective-permute-start.21 = (bf16[4,2,2,32,1536]{4,3,2,1,0:T(8,128)(2,1)}, bf16[4,2,2,32,1536]{4,3,2,1,0:T(8,128)(2,1)}, u32[]{:S(2)}, u32[]{:S(2)}) collective-permute-start(bf16[4,2,2,32,1536]{4,3,2,1,0:T(8,128)(2,1)} %bitcast.40), channel_id=1, source_target_pairs={{0,4},{4,0},{8,12},{12,8},{16,20},{20,16},{24,28},{28,24},{1,5},{5... | collective-permute-start | bytes 4718600 | tf_op jit(solution)/shard_map/ppermute | solution.py:706
  448.6 11.6 %collective-permute-start.19 = (bf16[4,2,2,16,1024]{4,3,2,1,0:T(8,128)(2,1)}, bf16[4,2,2,16,1024]{4,3,2,1,0:T(8,128)(2,1)}, u32[]{:S(2)}, u32[]{:S(2)}) collective-permute-start(bf16[4,2,2,16,1024]{4,3,2,1,0:T(8,128)(2,1)} %get-tuple-element.215), channel_id=1, source_target_pairs={{0,4},{4,0},{8,12},{12,8},{16,20},{20,16},{24,28},{28,24},{1,5},{5... | collective-permute-start | bytes 1572872 | tf_op jit(solution)/shard_map/ppermute | solution.py:706
  460.2 37.1 %collective-permute-start.16 = (bf16[144,1536]{1,0:T(8,128)(2,1)}, bf16[144,1536]{1,0:T(8,128)(2,1)}, u32[]{:S(2)}, u32[]{:S(2)}) collective-permute-start(bf16[144,1536]{1,0:T(8,128)(2,1)} %get-tuple-element.91), channel_id=1, source_target_pairs={{3,0},{7,4},{11,8},{15,12},{19,16},{23,20},{27,24},{31,28}} | collective-permute-start | bytes 1327112 | tf_op jit(solution)/shard_map/ppermute | solution.py:701
  461.5 37.9 %collective-permute-start.15 = (bf16[144,1536]{1,0:T(8,128)(2,1)}, bf16[144,1536]{1,0:T(8,128)(2,1)}, u32[]{:S(2)}, u32[]{:S(2)}) collective-permute-start(bf16[144,1536]{1,0:T(8,128)(2,1)} %get-tuple-element.91), channel_id=1, source_target_pairs={{2,0},{3,1},{6,4},{7,5},{10,8},{11,9},{14,12},{15,13},{18,16},{19,... | collective-permute-start | bytes 1327112 | tf_op jit(solution)/shard_map/ppermute | solution.py:701
  467.7 37.1 %collective-permute-start.27 = (bf16[2,2,896,128]{3,2,1,0:T(8,128)(2,1)}, bf16[2,2,896,128]{3,2,1,0:T(8,128)(2,1)}, u32[]{:S(2)}, u32[]{:S(2)}) collective-permute-start(bf16[2,2,896,128]{3,2,1,0:T(8,128)(2,1)} %get-tuple-element.102), channel_id=1, source_target_pairs={{0,2},{1,3},{2,0},{3,1},{4,6},{5,7},{6,4},{7,5},{8,10},{9,11},{10,... | collective-permute-start | bytes 2752520 | tf_op jit(solution)/shard_map/ppermute | solution.py:706
  471.1 33.7 %collective-permute-start.28 = (bf16[2,2,896,128]{3,2,1,0:T(8,128)(2,1)}, bf16[2,2,896,128]{3,2,1,0:T(8,128)(2,1)}, u32[]{:S(2)}, u32[]{:S(2)}) collective-permute-start(bf16[2,2,896,128]{3,2,1,0:T(8,128)(2,1)} %get-tuple-element.104), channel_id=1, source_target_pairs={{0,1},{1,0},{2,3},{3,2},{4,5},{5,4},{6,7},{7,6},{8,9},{9,8},{10,11... | collective-permute-start | bytes 2752520 | tf_op jit(solution)/shard_map/ppermute | solution.py:706
  483.6 20.7 %collective-permute-start.14 = (bf16[144,1536]{1,0:T(8,128)(2,1)}, bf16[144,1536]{1,0:T(8,128)(2,1)S(1)}, u32[]{:S(2)}, u32[]{:S(2)}) collective-permute-start(bf16[144,1536]{1,0:T(8,128)(2,1)} %get-tuple-element.91), channel_id=1, source_target_pairs={{1,0},{2,1},{3,2},{5,4},{6,5},{7,6},{9,8},{10,9},{11,10},{13,12},{... | collective-permute-start | bytes 1327112 | tf_op jit(solution)/shard_map/ppermute | solution.py:701
  497.3 69.5 %collective-permute-start.17 = (bf16[2,2,1536,128]{3,2,1,0:T(8,128)(2,1)}, bf16[2,2,1536,128]{3,2,1,0:T(8,128)(2,1)S(1)}, u32[]{:S(2)}, u32[]{:S(2)}) collective-permute-start(bf16[2,2,1536,128]{3,2,1,0:T(8,128)(2,1)} %get-tuple-element.92), channel_id=1, source_target_pairs={{0,2},{1,3},{2,0},{3,1},{4,6},{5,7},{6,4},{7,5},{8,10},{9,11},{10,... | collective-permute-start | bytes 4718600 | tf_op jit(solution)/shard_map/ppermute | solution.py:706
  499.5 67.3 %collective-permute-start.18 = (bf16[2,2,1536,128]{3,2,1,0:T(8,128)(2,1)}, bf16[2,2,1536,128]{3,2,1,0:T(8,128)(2,1)}, u32[]{:S(2)}, u32[]{:S(2)}) collective-permute-start(bf16[2,2,1536,128]{3,2,1,0:T(8,128)(2,1)} %get-tuple-element.94), channel_id=1, source_target_pairs={{0,1},{1,0},{2,3},{3,2},{4,5},{5,4},{6,7},{7,6},{8,9},{9,8},{10,11... | collective-permute-start | bytes 4718600 | tf_op jit(solution)/shard_map/ppermute | solution.py:706
  508.0 38.8 %collective-permute-start.29 = (bf16[2,896,128]{2,1,0:T(8,128)(2,1)}, bf16[2,896,128]{2,1,0:T(8,128)(2,1)S(1)}, u32[]{:S(2)}, u32[]{:S(2)}) collective-permute-start(bf16[2,896,128]{2,1,0:T(8,128)(2,1)} %get-tuple-element.106), channel_id=1, source_target_pairs={{0,1},{1,0},{2,3},{3,2},{4,5},{5,4},{6,7},{7,6},{8,9},{9,8},{10,11... | collective-permute-start | bytes 1376264 | tf_op jit(solution)/shard_map/ppermute | solution.py:706
  511.2 37.8 %collective-permute-start.30 = (bf16[2,896,128]{2,1,0:T(8,128)(2,1)}, bf16[2,896,128]{2,1,0:T(8,128)(2,1)}, u32[]{:S(2)}, u32[]{:S(2)}) collective-permute-start(bf16[2,896,128]{2,1,0:T(8,128)(2,1)} %get-tuple-element.108), channel_id=1, source_target_pairs={{0,2},{1,3},{2,0},{3,1},{4,6},{5,7},{6,4},{7,5},{8,10},{9,11},{10,... | collective-permute-start | bytes 1376264 | tf_op jit(solution)/shard_map/ppermute | solution.py:706
  526.2 27.9 %collective-permute-start.13 = (bf16[2,512,128]{2,1,0:T(8,128)(2,1)}, bf16[2,512,128]{2,1,0:T(8,128)(2,1)S(1)}, u32[]{:S(2)}, u32[]{:S(2)}) collective-permute-start(bf16[2,512,128]{2,1,0:T(8,128)(2,1)} %get-tuple-element.211), channel_id=1, source_target_pairs={{3,0},{7,4},{11,8},{15,12},{19,16},{23,20},{27,24},{31,28}} | collective-permute-start | bytes 786440 | tf_op jit(solution)/shard_map/ppermute | solution.py:701
  546.8 12.8 %collective-permute-start.12 = (bf16[2,512,128]{2,1,0:T(8,128)(2,1)}, bf16[2,512,128]{2,1,0:T(8,128)(2,1)}, u32[]{:S(2)}, u32[]{:S(2)}) collective-permute-start(bf16[2,512,128]{2,1,0:T(8,128)(2,1)} %get-tuple-element.212), channel_id=1, source_target_pairs={{2,0},{3,1},{6,4},{7,5},{10,8},{11,9},{14,12},{15,13},{18,16},{19,... | collective-permute-start | bytes 786440 | tf_op jit(solution)/shard_map/ppermute | solution.py:701
  548.9 12.6 %collective-permute-start.11 = (bf16[2,512,128]{2,1,0:T(8,128)(2,1)}, bf16[2,512,128]{2,1,0:T(8,128)(2,1)}, u32[]{:S(2)}, u32[]{:S(2)}) collective-permute-start(bf16[2,512,128]{2,1,0:T(8,128)(2,1)} %get-tuple-element.210), channel_id=1, source_target_pairs={{1,0},{2,1},{3,2},{5,4},{6,5},{7,6},{9,8},{10,9},{11,10},{13,12},{... | collective-permute-start | bytes 786440 | tf_op jit(solution)/shard_map/ppermute | solution.py:701
  554.1 88.6 %collective-permute-start.31 = (bf16[896,128]{1,0:T(8,128)(2,1)}, bf16[896,128]{1,0:T(8,128)(2,1)}, u32[]{:S(2)}, u32[]{:S(2)}) collective-permute-start(bf16[896,128]{1,0:T(8,128)(2,1)} %get-tuple-element.110), channel_id=1, source_target_pairs={{0,8},{4,12},{8,16},{12,20},{16,24},{20,28},{24,0},{28,4},{1,9},{5... | collective-permute-start | bytes 688136 | tf_op jit(solution)/shard_map/ppermute | solution.py:877
  559.6 85.3 %collective-permute-start.32 = (bf16[896,128]{1,0:T(8,128)(2,1)}, bf16[896,128]{1,0:T(8,128)(2,1)}, u32[]{:S(2)}, u32[]{:S(2)}) collective-permute-start(bf16[896,128]{1,0:T(8,128)(2,1)} %get-tuple-element.111), channel_id=1, source_target_pairs={{0,16},{4,20},{8,24},{12,28},{16,0},{20,4},{24,8},{28,12},{1,17},{... | collective-permute-start | bytes 688136 | tf_op jit(solution)/shard_map/ppermute | solution.py:877
  611.1 19.5 %collective-permute-start.38 = (bf16[4,2,2,32,1816]{4,3,2,1,0:T(8,128)(2,1)}, bf16[4,2,2,32,1816]{4,3,2,1,0:T(8,128)(2,1)}, u32[]{:S(2)}, u32[]{:S(2)}) collective-permute-start(bf16[4,2,2,32,1816]{4,3,2,1,0:T(8,128)(2,1)} %bitcast.124), channel_id=1, source_target_pairs={{0,4},{4,0},{8,12},{12,8},{16,20},{20,16},{24,28},{28,24},{1,5},{5... | collective-permute-start | bytes 5578760 | tf_op jit(solution)/shard_map/ppermute | solution.py:706
  614.0 14.0 %collective-permute-start.37 = (bf16[4,2,2,32,768]{4,3,2,1,0:T(8,128)(2,1)}, bf16[4,2,2,32,768]{4,3,2,1,0:T(8,128)(2,1)}, u32[]{:S(2)}, u32[]{:S(2)}) collective-permute-start(bf16[4,2,2,32,768]{4,3,2,1,0:T(8,128)(2,1)} %bitcast.47), channel_id=1, source_target_pairs={{0,4},{4,0},{8,12},{12,8},{16,20},{20,16},{24,28},{28,24},{1,5},{5... | collective-permute-start | bytes 2359304 | tf_op jit(solution)/shard_map/ppermute | solution.py:706
  627.9 17.0 %collective-permute-start.22 = (f32[2120]{0:T(1024)S(1)}, f32[2120]{0:T(1024)S(1)}, u32[]{:S(2)}, u32[]{:S(2)}) collective-permute-start(f32[2120]{0:T(1024)S(1)} %concatenate.22), channel_id=1, source_target_pairs={{0,4},{4,0},{8,12},{12,8},{16,20},{20,16},{24,28},{28,24},{1,5},{5... | collective-permute-start | bytes 25448 | tf_op jit(solution)/shard_map/ppermute | solution.py:706
  628.0 33.2 %collective-permute-start.49 = (bf16[2,1536,128]{2,1,0:T(8,128)(2,1)}, bf16[2,1536,128]{2,1,0:T(8,128)(2,1)}, u32[]{:S(2)}, u32[]{:S(2)}) collective-permute-start(bf16[2,1536,128]{2,1,0:T(8,128)(2,1)} %get-tuple-element.130), channel_id=1, source_target_pairs={{0,1},{1,0},{2,3},{3,2},{4,5},{5,4},{6,7},{7,6},{8,9},{9,8},{10,11... | collective-permute-start | bytes 2359304 | tf_op jit(solution)/shard_map/ppermute | solution.py:706
  630.6 31.0 %collective-permute-start.50 = (bf16[2,1536,128]{2,1,0:T(8,128)(2,1)}, bf16[2,1536,128]{2,1,0:T(8,128)(2,1)}, u32[]{:S(2)}, u32[]{:S(2)}) collective-permute-start(bf16[2,1536,128]{2,1,0:T(8,128)(2,1)} %get-tuple-element.132), channel_id=1, source_target_pairs={{0,2},{1,3},{2,0},{3,1},{4,6},{5,7},{6,4},{7,5},{8,10},{9,11},{10,... | collective-permute-start | bytes 2359304 | tf_op jit(solution)/shard_map/ppermute | solution.py:706
  642.8 23.3 %collective-permute-start.39 = (bf16[2,2,672,128]{3,2,1,0:T(8,128)(2,1)}, bf16[2,2,672,128]{3,2,1,0:T(8,128)(2,1)}, u32[]{:S(2)}, u32[]{:S(2)}) collective-permute-start(bf16[2,2,672,128]{3,2,1,0:T(8,128)(2,1)} %get-tuple-element.115), channel_id=1, source_target_pairs={{0,2},{1,3},{2,0},{3,1},{4,6},{5,7},{6,4},{7,5},{8,10},{9,11},{10,... | collective-permute-start | bytes 2064392 | tf_op jit(solution)/shard_map/ppermute | solution.py:706
  644.8 25.0 %collective-permute-start.40 = (bf16[2,2,672,128]{3,2,1,0:T(8,128)(2,1)}, bf16[2,2,672,128]{3,2,1,0:T(8,128)(2,1)}, u32[]{:S(2)}, u32[]{:S(2)}) collective-permute-start(bf16[2,2,672,128]{3,2,1,0:T(8,128)(2,1)} %get-tuple-element.117), channel_id=1, source_target_pairs={{0,1},{1,0},{2,3},{3,2},{4,5},{5,4},{6,7},{7,6},{8,9},{9,8},{10,11... | collective-permute-start | bytes 2064392 | tf_op jit(solution)/shard_map/ppermute | solution.py:706
  644.9 3.7 collective-permute-start.23
  648.7 6.3 collective-permute-start.33
  654.9 4.6 collective-permute-start.24
  659.5 13.7 %collective-permute-start.34 = (bf16[896,128]{1,0:T(8,128)(2,1)}, bf16[896,128]{1,0:T(8,128)(2,1)S(1)}, u32[]{:S(2)}, u32[]{:S(2)}) collective-permute-start(bf16[896,128]{1,0:T(8,128)(2,1)} %total.3.refs_0_), channel_id=1, source_target_pairs={{0,1},{1,0},{2,3},{3,2},{4,5},{5,4},{6,7},{7,6},{8,9},{9,8},{10,11... | collective-permute-start | bytes 688136 | tf_op jit(solution)/shard_map/ppermute | solution.py:706
  661.2 14.8 %collective-permute-start.35 = (bf16[896,128]{1,0:T(8,128)(2,1)}, bf16[896,128]{1,0:T(8,128)(2,1)}, u32[]{:S(2)}, u32[]{:S(2)}) collective-permute-start(bf16[896,128]{1,0:T(8,128)(2,1)} %total.3.refs_0_), channel_id=1, source_target_pairs={{0,2},{1,3},{2,0},{3,1},{4,6},{5,7},{6,4},{7,5},{8,10},{9,11},{10,... | collective-permute-start | bytes 688136 | tf_op jit(solution)/shard_map/ppermute | solution.py:706
  661.6 15.4 %collective-permute-start.36 = (bf16[896,128]{1,0:T(8,128)(2,1)}, bf16[896,128]{1,0:T(8,128)(2,1)}, u32[]{:S(2)}, u32[]{:S(2)}) collective-permute-start(bf16[896,128]{1,0:T(8,128)(2,1)} %total.3.refs_0_), channel_id=1, source_target_pairs={{0,3},{1,2},{2,1},{3,0},{4,7},{5,6},{6,5},{7,4},{8,11},{9,10},{10,... | collective-permute-start | bytes 688136 | tf_op jit(solution)/shard_map/ppermute | solution.py:706
  666.0 12.6 %collective-permute-start.25 = (f32[2120]{0:T(1024)S(1)}, f32[2120]{0:T(1024)S(1)}, u32[]{:S(2)}, u32[]{:S(2)}) collective-permute-start(f32[2120]{0:T(1024)S(1)} %add.287), channel_id=1, source_target_pairs={{0,1},{1,0},{2,3},{3,2},{4,5},{5,4},{6,7},{7,6},{8,9},{9,8},{10,11... | collective-permute-start | bytes 25448 | tf_op jit(solution)/shard_map/ppermute | solution.py:706
  669.9 17.1 %collective-permute-start.51 = (bf16[1536,128]{1,0:T(8,128)(2,1)}, bf16[1536,128]{1,0:T(8,128)(2,1)S(1)}, u32[]{:S(2)}, u32[]{:S(2)}) collective-permute-start(bf16[1536,128]{1,0:T(8,128)(2,1)} %get-tuple-element.134), channel_id=1, source_target_pairs={{0,8},{4,12},{8,16},{12,20},{16,24},{20,28},{24,0},{28,4},{1,9},{5... | collective-permute-start | bytes 1179656 | tf_op jit(solution)/shard_map/ppermute | solution.py:877
  673.3 25.4 %collective-permute-start.52 = (bf16[1536,128]{1,0:T(8,128)(2,1)}, bf16[1536,128]{1,0:T(8,128)(2,1)S(1)}, u32[]{:S(2)}, u32[]{:S(2)}) collective-permute-start(bf16[1536,128]{1,0:T(8,128)(2,1)} %get-tuple-element.135), channel_id=1, source_target_pairs={{0,16},{4,20},{8,24},{12,28},{16,0},{20,4},{24,8},{28,12},{1,17},{... | collective-permute-start | bytes 1179656 | tf_op jit(solution)/shard_map/ppermute | solution.py:877
  676.0 22.7 %collective-permute-start.53 = (bf16[1536,128]{1,0:T(8,128)(2,1)}, bf16[1536,128]{1,0:T(8,128)(2,1)S(1)}, u32[]{:S(2)}, u32[]{:S(2)}) collective-permute-start(bf16[1536,128]{1,0:T(8,128)(2,1)} %get-tuple-element.136), channel_id=1, source_target_pairs={{0,24},{4,28},{8,0},{12,4},{16,8},{20,12},{24,16},{28,20},{1,25},{... | collective-permute-start | bytes 1179656 | tf_op jit(solution)/shard_map/ppermute | solution.py:877
  677.0 26.3 %collective-permute-start.41 = (bf16[2,672,128]{2,1,0:T(8,128)(2,1)}, bf16[2,672,128]{2,1,0:T(8,128)(2,1)S(1)}, u32[]{:S(2)}, u32[]{:S(2)}) collective-permute-start(bf16[2,672,128]{2,1,0:T(8,128)(2,1)} %get-tuple-element.119), channel_id=1, source_target_pairs={{0,1},{1,0},{2,3},{3,2},{4,5},{5,4},{6,7},{7,6},{8,9},{9,8},{10,11... | collective-permute-start | bytes 1032200 | tf_op jit(solution)/shard_map/ppermute | solution.py:706
  678.7 24.6 %collective-permute-start.42 = (bf16[2,672,128]{2,1,0:T(8,128)(2,1)}, bf16[2,672,128]{2,1,0:T(8,128)(2,1)S(1)}, u32[]{:S(2)}, u32[]{:S(2)}) collective-permute-start(bf16[2,672,128]{2,1,0:T(8,128)(2,1)} %get-tuple-element.121), channel_id=1, source_target_pairs={{0,2},{1,3},{2,0},{3,1},{4,6},{5,7},{6,4},{7,5},{8,10},{9,11},{10,... | collective-permute-start | bytes 1032200 | tf_op jit(solution)/shard_map/ppermute | solution.py:706
  684.2 31.1 %copy-start.9 = (bf16[512,1024]{1,0:T(8,128)(2,1)S(1)}, bf16[512,1024]{1,0:T(8,128)(2,1)}, u32[]{:S(2)}) copy-start(bf16[512,1024]{1,0:T(8,128)(2,1)} %param.27) | copy-start | bytes 3145732
  687.0 32.1 %collective-permute-start.26 = (f32[2120]{0:T(1024)S(1)}, f32[2120]{0:T(1024)S(1)}, u32[]{:S(2)}, u32[]{:S(2)}) collective-permute-start(f32[2120]{0:T(1024)S(1)} %add.288), channel_id=1, source_target_pairs={{0,2},{1,3},{2,0},{3,1},{4,6},{5,7},{6,4},{7,5},{8,10},{9,11},{10,... | collective-permute-start | bytes 25448 | tf_op jit(solution)/shard_map/ppermute | solution.py:706
  701.9 33.8 %collective-permute-start.54 = (bf16[1536,128]{1,0:T(8,128)(2,1)}, bf16[1536,128]{1,0:T(8,128)(2,1)S(1)}, u32[]{:S(2)}, u32[]{:S(2)}) collective-permute-start(bf16[1536,128]{1,0:T(8,128)(2,1)} %total.5.refs_0_), channel_id=1, source_target_pairs={{0,1},{1,0},{2,3},{3,2},{4,5},{5,4},{6,7},{7,6},{8,9},{9,8},{10,11... | collective-permute-start | bytes 1179656 | tf_op jit(solution)/shard_map/ppermute | solution.py:706
  706.6 15.0 %collective-permute-start.43 = (bf16[672,128]{1,0:T(8,128)(2,1)}, bf16[672,128]{1,0:T(8,128)(2,1)S(1)}, u32[]{:S(2)}, u32[]{:S(2)}) collective-permute-start(bf16[672,128]{1,0:T(8,128)(2,1)} %get-tuple-element.123), channel_id=1, source_target_pairs={{0,8},{4,12},{8,16},{12,20},{16,24},{20,28},{24,0},{28,4},{1,9},{5... | collective-permute-start | bytes 516104 | tf_op jit(solution)/shard_map/ppermute | solution.py:877
  719.2 20.3 %collective-permute-start.55 = (bf16[1536,128]{1,0:T(8,128)(2,1)S(1)}, bf16[1536,128]{1,0:T(8,128)(2,1)S(1)}, u32[]{:S(2)}, u32[]{:S(2)}) collective-permute-start(bf16[1536,128]{1,0:T(8,128)(2,1)S(1)} %copy-done.15), channel_id=1, source_target_pairs={{0,2},{1,3},{2,0},{3,1},{4,6},{5,7},{6,4},{7,5},{8,10},{9,11},{10,... | collective-permute-start | bytes 1179656 | tf_op jit(solution)/shard_map/ppermute | solution.py:706
  719.9 19.7 %collective-permute-start.56 = (bf16[1536,128]{1,0:T(8,128)(2,1)S(1)}, bf16[1536,128]{1,0:T(8,128)(2,1)S(1)}, u32[]{:S(2)}, u32[]{:S(2)}) collective-permute-start(bf16[1536,128]{1,0:T(8,128)(2,1)S(1)} %copy-done.15), channel_id=1, source_target_pairs={{0,3},{1,2},{2,1},{3,0},{4,7},{5,6},{6,5},{7,4},{8,11},{9,10},{10,... | collective-permute-start | bytes 1179656 | tf_op jit(solution)/shard_map/ppermute | solution.py:706
  721.4 9.8 %collective-permute-start.44 = (bf16[672,128]{1,0:T(8,128)(2,1)S(1)}, bf16[672,128]{1,0:T(8,128)(2,1)S(1)}, u32[]{:S(2)}, u32[]{:S(2)}) collective-permute-start(bf16[672,128]{1,0:T(8,128)(2,1)S(1)} %copy-done.58), channel_id=1, source_target_pairs={{0,16},{4,20},{8,24},{12,28},{16,0},{20,4},{24,8},{28,12},{1,17},{... | collective-permute-start | bytes 516104 | tf_op jit(solution)/shard_map/ppermute | solution.py:877
  721.6 9.5 %collective-permute-start.45 = (bf16[672,128]{1,0:T(8,128)(2,1)S(1)}, bf16[672,128]{1,0:T(8,128)(2,1)S(1)}, u32[]{:S(2)}, u32[]{:S(2)}) collective-permute-start(bf16[672,128]{1,0:T(8,128)(2,1)S(1)} %copy-done.57), channel_id=1, source_target_pairs={{0,24},{4,28},{8,0},{12,4},{16,8},{20,12},{24,16},{28,20},{1,25},{... | collective-permute-start | bytes 516104 | tf_op jit(solution)/shard_map/ppermute | solution.py:877
  733.8 10.4 %collective-permute-start.46 = (bf16[672,128]{1,0:T(8,128)(2,1)}, bf16[672,128]{1,0:T(8,128)(2,1)S(1)}, u32[]{:S(2)}, u32[]{:S(2)}) collective-permute-start(bf16[672,128]{1,0:T(8,128)(2,1)} %total.4.refs_0_), channel_id=1, source_target_pairs={{0,1},{1,0},{2,3},{3,2},{4,5},{5,4},{6,7},{7,6},{8,9},{9,8},{10,11... | collective-permute-start | bytes 516104 | tf_op jit(solution)/shard_map/ppermute | solution.py:706
  735.1 10.4 %collective-permute-start.47 = (bf16[672,128]{1,0:T(8,128)(2,1)}, bf16[672,128]{1,0:T(8,128)(2,1)S(1)}, u32[]{:S(2)}, u32[]{:S(2)}) collective-permute-start(bf16[672,128]{1,0:T(8,128)(2,1)} %total.4.refs_0_), channel_id=1, source_target_pairs={{0,2},{1,3},{2,0},{3,1},{4,6},{5,7},{6,4},{7,5},{8,10},{9,11},{10,... | collective-permute-start | bytes 516104 | tf_op jit(solution)/shard_map/ppermute | solution.py:706
  735.7 9.8 %collective-permute-start.48 = (bf16[672,128]{1,0:T(8,128)(2,1)}, bf16[672,128]{1,0:T(8,128)(2,1)S(1)}, u32[]{:S(2)}, u32[]{:S(2)}) collective-permute-start(bf16[672,128]{1,0:T(8,128)(2,1)} %total.4.refs_0_), channel_id=1, source_target_pairs={{0,3},{1,2},{2,1},{3,0},{4,7},{5,6},{6,5},{7,4},{8,11},{9,10},{10,... | collective-permute-start | bytes 516104 | tf_op jit(solution)/shard_map/ppermute | solution.py:706
  (62 other events, 397.7 us)
Sparse Core Ops, SparseCore 0:
  11.5 64.7 all-gather.13
  79.7 77.0 all-gather.5
  159.7 64.4 all-gather.9
  227.1 56.2 all-gather.7
  286.6 76.4 all-gather.11
